TPU v7x, 256 devices: a whole 4x4x8 slice. The times are simulated.
256 devices in a mesh: lvl: 2 (over z_hi), tile: 128 (over x, z_lo, y, core).
Axes of the slice: x: 4, y: 4, z: 8 (z_hi: 2, z_lo: 4; z = z_hi * 4 + z_lo), core: 2. Of those that a mesh axis runs over, the one named last changes fastest.
Arguments:
- velocity: float32 [3, 4, 512, 512], P(None, None, 'tile'), may hold values from -3 to 3
- dumbbells: float32 [2, 3, 8, 4, 512, 512], P('lvl', None, None, None, 'tile'), may hold values from -2.97 to 2.97, as said below
- increments: bfloat16 [2, 2, 3, 8, 4, 512, 512], P('lvl', None, None, None, None, 'tile'), may hold values from -5 to 5
Outputs:
- velocity_next: float32 [3, 4, 512, 512], P(None, None, 'tile')
- stress: float32 [6, 4, 512, 512], P(None, None, 'tile')
- dumbbells_next: float32 [2, 3, 8, 4, 512, 512], P('lvl', None, None, None, 'tile')
Inputs may be any that keep to these rules, and one draw needn't show every extreme that they name: `dumbbells`: every dumbbell's length is at most 2.97.
All inputs are finite; a program needn't handle non-finite values.
Results may differ from a plain program's by a relative error of at most 0.0006.
Values sent between devices are 32-bit elements; how exact they have to be, the bound alone decides.
No kernel may reach another device: no remote copies, remote signals or barrier semaphores. Data moves between devices by JAX's collectives and lax.ppermute only.
A program may use at most 64 MiB of HBM per device.

v0:
```python
import math

import jax
import jax.numpy as jnp
from jax import lax
from jax.sharding import PartitionSpec as P

STEP_TIME = 0.25
WEISSENBERG = 1.0
SPRING_LIMIT = 10.0
RADIUS_CAP = 3.0
VISCOSITY = 0.5
POLYMER_WEIGHT = 0.2
NOISE_GAIN = math.sqrt(STEP_TIME / (2.0 * WEISSENBERG))
COMPONENT = ((0, 3, 4), (3, 1, 5), (4, 5, 2))


def extended(cells, sides, width):
    for axis, dim in sides:
        count = lax.axis_size(axis)
        head = lax.slice_in_dim(cells, 0, width, axis=dim)
        tail = lax.slice_in_dim(cells, cells.shape[dim] - width, cells.shape[dim], axis=dim)
        cells = jnp.concatenate(
            [
                lax.ppermute(tail, axis, [(i, (i + 1) % count) for i in range(count)]),
                cells,
                lax.ppermute(head, axis, [((i + 1) % count, i) for i in range(count)]),
            ],
            axis=dim,
        )
    return cells


def advance(state, kappa, noise, span):
    spring = 1.0 / (
        1.0 - (state[0] * state[0] + state[1] * state[1] + state[2] * state[2]) / SPRING_LIMIT
    )
    moved = []
    for row_axis in range(3):
        stretch = (
            kappa[row_axis, 0][None] * state[0]
            + kappa[row_axis, 1][None] * state[1]
            + kappa[row_axis, 2][None] * state[2]
        )
        moved.append(
            state[row_axis]
            + span * (stretch - spring * state[row_axis] / (2.0 * WEISSENBERG))
            + NOISE_GAIN * noise[row_axis]
        )
    length2 = moved[0] * moved[0] + moved[1] * moved[1] + moved[2] * moved[2]
    factor = jnp.minimum(1.0, RADIUS_CAP / jnp.sqrt(jnp.maximum(length2, RADIUS_CAP * RADIUS_CAP)))
    return jnp.stack([entry * factor for entry in moved])


def kramers(state):
    spring = 1.0 / (
        1.0 - (state[0] * state[0] + state[1] * state[1] + state[2] * state[2]) / SPRING_LIMIT
    )
    return jnp.stack(
        [
            state[0] * state[0] * spring,
            state[1] * state[1] * spring,
            state[2] * state[2] * spring,
            state[0] * state[1] * spring,
            state[0] * state[2] * spring,
            state[1] * state[2] * spring,
        ]
    )


def coarsen(field):
    extent = field.shape
    leading = extent[:-3]
    blocked = field.reshape(leading + (extent[-3] // 2, 2, extent[-2] // 2, 2, extent[-1] // 2, 2))
    return jnp.mean(blocked, axis=(-5, -3, -1))


def spread(field):
    extent = field.shape
    leading = extent[:-3]
    widened = jnp.broadcast_to(
        field[..., :, None, :, None, :, None],
        leading + (extent[-3], 2, extent[-2], 2, extent[-1], 2),
    )
    return widened.reshape(leading + (2 * extent[-3], 2 * extent[-2], 2 * extent[-1]))


def finish(moments):
    identity = jnp.array([1.0, 1.0, 1.0, 0.0, 0.0, 0.0], jnp.float32).reshape(6, 1, 1, 1)
    return (moments - identity) / WEISSENBERG


def wall_pair(field):
    widths = [(0, 0)] * (field.ndim - 3) + [(1, 1), (0, 0), (0, 0)]
    padded = jnp.pad(field, widths)
    return (padded[..., 2:, :, :], padded[..., :-2, :, :])


def depth_pair(field):
    return (jnp.roll(field, -1, axis=-1), jnp.roll(field, 1, axis=-1))


def rim_pair(padded):
    return (padded[..., 2:, :], padded[..., :-2, :])


def velocity_terms(velocity, pairs):
    gradient = jnp.stack(
        [(pairs[direction][0] - pairs[direction][1]) * 0.5 for direction in range(3)], axis=1
    )
    laplace = (
        pairs[0][0]
        + pairs[0][1]
        + pairs[1][0]
        + pairs[1][1]
        + pairs[2][0]
        + pairs[2][1]
        - 6.0 * velocity
    )
    carried = (
        velocity[0][None] * gradient[:, 0]
        + velocity[1][None] * gradient[:, 1]
        + velocity[2][None] * gradient[:, 2]
    )
    return (gradient, laplace, carried)


def used_three(field):
    return jnp.stack([field[3], field[1], field[5]])


def stress_force(stress, rim_three):
    wall_side = wall_pair(stress)
    depth_side = depth_pair(stress)
    rim_side = rim_pair(rim_three)
    result_rows = []
    for row_axis in range(3):
        total_force = jnp.zeros_like(stress[0])
        total_force = (
            total_force
            + (wall_side[0][COMPONENT[row_axis][0]] - wall_side[1][COMPONENT[row_axis][0]]) * 0.5
        )
        total_force = total_force + (rim_side[0][row_axis] - rim_side[1][row_axis]) * 0.5
        total_force = (
            total_force
            + (depth_side[0][COMPONENT[row_axis][2]] - depth_side[1][COMPONENT[row_axis][2]]) * 0.5
        )
        result_rows.append(total_force)
    return jnp.stack(result_rows)


def cell_means(state):
    return coarsen(jnp.mean(kramers(state), axis=1))


def local(velocity, dumbbells, increments):
    padded = extended(velocity, (("tile", 2),), 1)
    gradient, laplace, carried = velocity_terms(
        velocity, [wall_pair(velocity), rim_pair(padded), depth_pair(velocity)]
    )
    kappa_coarse = spread(coarsen(gradient))
    own_state = dumbbells[0]
    first_half = increments[0, 0].astype(jnp.float32)
    second_half = increments[0, 1].astype(jnp.float32)
    both_halves = first_half + second_half
    level_index = lax.axis_index("lvl")

    def level_zero(operands):
        state, first, second, summed = operands
        advanced = advance(state, gradient, summed, STEP_TIME)
        return (advanced, finish(jnp.mean(kramers(advanced), axis=1)))

    def level_one(operands):
        state, first, second, summed = operands
        fine_path = advance(
            advance(state, kappa_coarse, first, 0.5 * STEP_TIME),
            kappa_coarse,
            second,
            0.5 * STEP_TIME,
        )
        coarse_path = advance(state, kappa_coarse, summed, STEP_TIME)
        correction = (cell_means(fine_path) - cell_means(coarse_path)) / WEISSENBERG
        return (fine_path, spread(correction))

    advanced_state, partial_value = lax.cond(
        level_index == 0, level_zero, level_one, (own_state, first_half, second_half, both_halves)
    )
    stress = lax.psum(partial_value, "lvl")
    stress_padded = extended(stress, (("tile", 2),), 1)
    rim_three = used_three(stress_padded)
    force = stress_force(stress, rim_three)
    velocity_next = velocity + STEP_TIME * (VISCOSITY * laplace - carried + POLYMER_WEIGHT * force)
    return (velocity_next, stress, advanced_state[None])


def solution(mesh):
    in_specs = (
        P(None, None, "tile", None),
        P("lvl", None, None, None, "tile", None),
        P("lvl", None, None, None, None, "tile", None),
    )
    out_specs = (
        P(None, None, "tile", None),
        P(None, None, "tile", None),
        P("lvl", None, None, None, "tile", None),
    )
    return jax.shard_map(local, mesh=mesh, in_specs=in_specs, out_specs=out_specs, check_vma=False)
```

profile of v0, /device:TPU:0, one launch (start us, length us, event | category | flops | bytes accessed | tf_op | source)
XLA Modules:
  0.0 189.4 jit_solution(1429423454079395701)
XLA Ops:
  7.2 1.0 fusion.49
  8.2 7.0 %collective-permute-start = (f32[3,4,1,512]{3,2,1,0:T(1,128)S(1)}, f32[3,4,1,512]{3,2,1,0:T(1,128)S(1)}, u32[]{:S(2)}, u32[]{:S(2)}) collective-permute-start(f32[3,4,1,512]{3,2,1,0:T(1,128)S(1)} %get-tuple-element.198), channel_id=1, source_target_pairs={{1,0},{2,1},{3,2},{4,3},{5,4},{6,5},{7,6},{8,7},{9,8},{10,9},{11,1... | collective-permute-start | bytes 73736 | tf_op jit(solution)/shard_map/ppermute | solution.py:27
  15.3 1.7 fusion.47
  17.0 1.4 fusion.48
  18.4 1.5 fusion.43
  22.1 7.7 %mul.1766 = f32[3,1,2,2,2,2,256,2]{7,6,5,4,3,2,0,1:T(8,128)} reshape(f32[3,1,4,4,512]{4,3,2,0,1:T(4,128)S(1)} %get-tuple-element.142) | data formatting | bytes 196608 | tf_op jit(solution)/shard_map/mul | solution.py:109
  29.8 5.1 %copy.44 = f32[3,1,2,2,2,2,256,2]{6,7,5,4,3,2,1,0:T(2,128)} copy(f32[3,1,2,2,2,2,256,2]{7,6,5,4,3,2,0,1:T(8,128)} %mul.1766) | data formatting | bytes 196608 | tf_op jit(solution)/shard_map/mul | solution.py:109
  35.1 7.7 %stack.41 = f32[3,1,2,2,2,2,256,2]{7,6,5,4,3,2,0,1:T(8,128)} reshape(f32[3,4,4,512]{3,2,1,0:T(4,128)S(1)} %get-tuple-element.195) | data formatting | bytes 196608 | tf_op jit(solution)/shard_map/stack | solution.py:108
  42.7 5.0 %copy.42 = f32[3,1,2,2,2,2,256,2]{6,7,5,4,3,2,1,0:T(2,128)} copy(f32[3,1,2,2,2,2,256,2]{7,6,5,4,3,2,0,1:T(8,128)} %stack.41) | data formatting | bytes 196608 | tf_op jit(solution)/shard_map/stack | solution.py:108
  47.8 7.6 %stack.42 = f32[3,1,2,2,2,2,256,2]{7,6,5,4,3,2,0,1:T(8,128)} reshape(f32[3,4,4,512]{3,2,1,0:T(4,128)S(1)} %get-tuple-element.196) | data formatting | bytes 196608 | tf_op jit(solution)/shard_map/stack | solution.py:108
  55.4 5.1 %copy.43 = f32[3,1,2,2,2,2,256,2]{6,7,5,4,3,2,1,0:T(2,128)} copy(f32[3,1,2,2,2,2,256,2]{7,6,5,4,3,2,0,1:T(8,128)} %stack.42) | data formatting | bytes 196608 | tf_op jit(solution)/shard_map/stack | solution.py:108
  60.5 1.2 pad_maximum_fusion
  61.7 10.0 %conditional.1 = (f32[6,4,4,512]{3,2,1,0:T(4,128)S(1)}, f32[1,3,8,4,4,512]{5,4,3,2,1,0:T(4,128)S(1)}) conditional(s32[]{:T(128)} %convert_element_type.19, (f32[3,8,4,4,512]{4,1,3,2,0:T(8,128)S(1)}, f32[3,3,2,2,2,2,256,2]{6,7,5,4,3,2,1,0:T(2,128)S(1)}, f32[3,8,4,4,512]{4,1,3,2,0:T(8,128)S(1)}, f32[3,8,4,4,512]{4,1,3,2,0:T(8,128)S(1)}, ...), branch_computations={%region_0.6_spmd, %region_6.8_spmd.clone} | conditional | flops 18790398 | bytes 33030180 | solution.py:185
  62.8 1.0 fusion.7
  64.1 1.1 multiply_dynamic-update-slice_fusion.17
  69.1 1.8 reduce_sum.60
  72.5 92.2 %all-reduce.4.cloned.1.call-done = f32[6,4,4,512]{3,2,1,0:T(4,128)} async-done(((f32[6,4,4,512]{3,2,1,0:T(4,128)}), f32[6,4,4,512]{3,2,1,0:T(4,128)}) %all-reduce.4.cloned.1.call-update) | async-done | bytes 196624 | tf_op jit(solution)/shard_map/psum | solution.py:188
  164.6 1.2 fusion.44
  165.8 4.4 %collective-permute-start.2 = (f32[6,4,1,512]{3,2,1,0:T(1,128)S(1)}, f32[6,4,1,512]{3,2,1,0:T(1,128)S(1)}, u32[]{:S(2)}, u32[]{:S(2)}) collective-permute-start(f32[6,4,1,512]{3,2,1,0:T(1,128)S(1)} %get-tuple-element.178), channel_id=1, source_target_pairs={{1,0},{2,1},{3,2},{4,3},{5,4},{6,5},{7,6},{8,7},{9,8},{10,9},{11,1... | collective-permute-start | bytes 147464 | tf_op jit(solution)/shard_map/ppermute | solution.py:27
  170.2 1.2 fusion.45
  171.4 0.9 fusion.46
  172.3 7.4 %collective-permute-done.3 = f32[6,4,1,512]{3,2,1,0:T(1,128)S(1)} collective-permute-done((f32[6,4,1,512]{3,2,1,0:T(1,128)S(1)}, f32[6,4,1,512]{3,2,1,0:T(1,128)S(1)}, u32[]{:S(2)}, u32[]{:S(2)}) %collective-permute-start.3) | collective-permute-done | bytes 49184 | tf_op jit(solution)/shard_map/ppermute | solution.py:25
  179.7 1.0 fusion.33
  180.9 0.9 fusion.16
  (58 shorter events, 9.6 us)
Async XLA Ops:
  7.2 157.5 %all-reduce.4.cloned.1.call-start = ((), (), s32[]{:S(2)}) async-start(), calls=%async_computation | async-start | bytes 393216 | tf_op jit(solution)/shard_map/psum | solution.py:188
  8.2 26.7 %collective-permute-start = (f32[3,4,1,512]{3,2,1,0:T(1,128)S(1)}, f32[3,4,1,512]{3,2,1,0:T(1,128)S(1)}, u32[]{:S(2)}, u32[]{:S(2)}) collective-permute-start(f32[3,4,1,512]{3,2,1,0:T(1,128)S(1)} %get-tuple-element.198), channel_id=1, source_target_pairs={{1,0},{2,1},{3,2},{4,3},{5,4},{6,5},{7,6},{8,7},{9,8},{10,9},{11,1... | collective-permute-start | bytes 73736 | tf_op jit(solution)/shard_map/ppermute | solution.py:27
  15.3 19.6 %collective-permute-start.1 = (f32[3,4,1,512]{3,2,1,0:T(1,128)S(1)}, f32[3,4,1,512]{3,2,1,0:T(1,128)S(1)}, u32[]{:S(2)}, u32[]{:S(2)}) collective-permute-start(f32[3,4,1,512]{3,2,1,0:T(1,128)S(1)} %get-tuple-element.197), channel_id=1, source_target_pairs={{0,1},{1,2},{2,3},{3,4},{4,5},{5,6},{6,7},{7,8},{8,9},{9,10},{10,1... | collective-permute-start | bytes 73736 | tf_op jit(solution)/shard_map/ppermute | solution.py:25
  20.4 1.3 copy-start.5
  29.8 5.1 %copy-start.1 = (f32[3,4,4,512]{3,2,1,0:T(4,128)S(1)}, f32[3,4,4,512]{3,2,1,0:T(4,128)}, u32[]{:S(2)}) copy-start(f32[3,4,4,512]{3,2,1,0:T(4,128)} %param.6) | copy-start | bytes 294916
  34.9 7.8 %copy-start.11 = (f32[3,4,1,512]{3,2,1,0:T(1,128)}, f32[3,4,1,512]{3,2,1,0:T(1,128)S(1)}, u32[]{:S(2)}) copy-start(f32[3,4,1,512]{3,2,1,0:T(1,128)S(1)} %collective-permute-done) | copy-start | bytes 73732
  34.9 7.8 %copy-start.13 = (f32[3,4,1,512]{3,2,1,0:T(1,128)}, f32[3,4,1,512]{3,2,1,0:T(1,128)S(1)}, u32[]{:S(2)}) copy-start(f32[3,4,1,512]{3,2,1,0:T(1,128)S(1)} %collective-permute-done.1) | copy-start | bytes 73732
  35.0 7.7 %copy-start.2 = (f32[3,4,4,512]{3,2,1,0:T(4,128)}, f32[3,4,4,512]{3,2,1,0:T(4,128)S(1)}, u32[]{:S(2)}) copy-start(f32[3,4,4,512]{3,2,1,0:T(4,128)S(1)} %get-tuple-element.195) | copy-start | bytes 294916
  35.1 12.7 %copy-start.3 = (f32[3,4,4,512]{3,2,1,0:T(4,128)}, f32[3,4,4,512]{3,2,1,0:T(4,128)S(1)}, u32[]{:S(2)}) copy-start(f32[3,4,4,512]{3,2,1,0:T(4,128)S(1)} %get-tuple-element.196) | copy-start | bytes 294916
  68.3 2.6 %copy-start.15 = (f32[6]{0:T(128)S(1)}, f32[6]{0:T(128)}, u32[]{:S(2)}) copy-start(f32[6]{0:T(128)} %constant.105) | copy-start | bytes 76 | tf_op jit(solution)/shard_map/cond
  71.7 0.7 copy-start.4
  71.7 109.2 %copy-start.6 = (f32[1,3,8,4,4,512]{5,4,3,2,1,0:T(4,128)}, f32[1,3,8,4,4,512]{5,4,3,2,1,0:T(4,128)S(1)}, u32[]{:S(2)}) copy-start(f32[1,3,8,4,4,512]{5,4,3,2,1,0:T(4,128)S(1)} %get-tuple-element.207) | copy-start | bytes 2359300
  72.4 108.5 %copy-start.7 = (f32[3,4,4,511]{3,2,1,0:T(4,128)S(1)}, f32[3,4,4,511]{3,2,1,0:T(4,128)}, u32[]{:S(2)}) copy-start(f32[3,4,4,511]{3,2,1,0:T(4,128)} %get-tuple-element.187) | copy-start | bytes 294340
  72.4 108.5 %copy-start.8 = (f32[3,4,4,511]{3,2,1,0:T(4,128)S(1)}, f32[3,4,4,511]{3,2,1,0:T(4,128)}, u32[]{:S(2)}) copy-start(f32[3,4,4,511]{3,2,1,0:T(4,128)} %get-tuple-element.190) | copy-start | bytes 294340
  72.4 108.5 %copy-start.9 = (f32[3,4,4,1]{3,2,1,0:T(4,128)S(1)}, f32[3,4,4,1]{3,2,1,0:T(4,128)}, u32[]{:S(2)}) copy-start(f32[3,4,4,1]{3,2,1,0:T(4,128)} %get-tuple-element.191) | copy-start | bytes 580
  72.4 108.5 %copy-start.10 = (f32[3,4,4,1]{3,2,1,0:T(4,128)S(1)}, f32[3,4,4,1]{3,2,1,0:T(4,128)}, u32[]{:S(2)}) copy-start(f32[3,4,4,1]{3,2,1,0:T(4,128)} %get-tuple-element.194) | copy-start | bytes 580
  72.4 108.5 %copy-start.12 = (f32[3,4,1,512]{3,2,1,0:T(1,128)S(1)}, f32[3,4,1,512]{3,2,1,0:T(1,128)}, u32[]{:S(2)}) copy-start(f32[3,4,1,512]{3,2,1,0:T(1,128)} %copy-done.11) | copy-start | bytes 73732
  72.4 108.5 %copy-start.14 = (f32[3,4,1,512]{3,2,1,0:T(1,128)S(1)}, f32[3,4,1,512]{3,2,1,0:T(1,128)}, u32[]{:S(2)}) copy-start(f32[3,4,1,512]{3,2,1,0:T(1,128)} %copy-done.13) | copy-start | bytes 73732
  164.6 16.1 %copy-start = (f32[6,4,4,512]{3,2,1,0:T(4,128)S(1)}, f32[6,4,4,512]{3,2,1,0:T(4,128)}, u32[]{:S(2)}) copy-start(f32[6,4,4,512]{3,2,1,0:T(4,128)} %all-reduce.4.cloned.1.call-done) | copy-start | bytes 589828
  165.8 6.5 %collective-permute-start.2 = (f32[6,4,1,512]{3,2,1,0:T(1,128)S(1)}, f32[6,4,1,512]{3,2,1,0:T(1,128)S(1)}, u32[]{:S(2)}, u32[]{:S(2)}) collective-permute-start(f32[6,4,1,512]{3,2,1,0:T(1,128)S(1)} %get-tuple-element.178), channel_id=1, source_target_pairs={{1,0},{2,1},{3,2},{4,3},{5,4},{6,5},{7,6},{8,7},{9,8},{10,9},{11,1... | collective-permute-start | bytes 147464 | tf_op jit(solution)/shard_map/ppermute | solution.py:27
  170.2 9.5 %collective-permute-start.3 = (f32[6,4,1,512]{3,2,1,0:T(1,128)S(1)}, f32[6,4,1,512]{3,2,1,0:T(1,128)S(1)}, u32[]{:S(2)}, u32[]{:S(2)}) collective-permute-start(f32[6,4,1,512]{3,2,1,0:T(1,128)S(1)} %get-tuple-element.179), channel_id=1, source_target_pairs={{0,1},{1,2},{2,3},{3,4},{4,5},{5,6},{6,7},{7,8},{8,9},{9,10},{10,1... | collective-permute-start | bytes 147464 | tf_op jit(solution)/shard_map/ppermute | solution.py:25
Sparse Core Ops, SparseCore 0:
  72.5 92.0 all-reduce.3
where the time goes:
time: 190 us; the launch traced here: 189 us
  waiting for transfers between devices  99.6 us (52%)
  local copies, waits for them, and re-layouts  50.3 us (26%)
  between operations  14.3 us (8%)
  other arithmetic  13.3 us (7%)
  starting transfers between devices  11.5 us (6%)
    psum x1, waiting for transfers between devices, local(): stress = lax.psum(partial_value, 'lvl')  92.2 us
    another operation x4, local copies, waits for them, and re-layouts, velocity_terms(): jnp.stack([(pairs[direction][0] - pairs[direction][1]) * 0.5 for directio...  25.4 us
    mul x2, local copies, waits for them, and re-layouts, velocity_terms(): (pairs[direction][0] - pairs[direction][1]) * 0.5  12.8 us
    ppermute x2, starting transfers between devices, extended(): lax.ppermute(head, axis, [((i + 1) % count, i) for i in range(count)])  11.5 us
    ppermute x2, waiting for transfers between devices, extended(): lax.ppermute(tail, axis, [(i, (i + 1) % count) for i in range(count)])  7.42 us
    slice x4, local copies, waits for them, and re-layouts, depth_pair(): return (jnp.roll(field, -1, axis=-1), jnp.roll(field, 1, axis=-1))  5.27 us
    cond x5, other arithmetic  4.27 us
  transfers between devices with their start and end apart: 5, of which 2 were waited for; matrix products, arithmetic and copies ran while one was open for 11% of the time, Pallas kernels for 0%

commit v1 on v0

v1 whole, which is shorter than its diff:
```python
import functools
import math

import jax
import jax.numpy as jnp
from jax import lax
from jax.experimental import pallas as pl
from jax.experimental.pallas import tpu as pltpu
from jax.sharding import PartitionSpec as P

STEP_TIME = 0.25
SPRING_LIMIT = 10.0
RADIUS_CAP = 3.0
VISCOSITY = 0.5
POLYMER_WEIGHT = 0.2
NOISE_GAIN = math.sqrt(STEP_TIME / 2.0)
PLANES = 4
SAMPLES = 8
PAIRS = ((0, 0), (1, 1), (2, 2), (0, 1), (0, 2), (1, 2))
RIM = (3, 1, 5)
REST = (0, 2, 4)
F32 = jnp.float32


def view(field):
    lead = field.shape[:-2]
    split = field.reshape(lead + (4, 4, 128))
    return jnp.swapaxes(split, -3, -2).reshape(lead + (16, 128))


def unview(field):
    lead = field.shape[:-2]
    split = field.reshape(lead + (4, 4, 128))
    return jnp.swapaxes(split, -3, -2).reshape(lead + (4, 512))


def row_of():
    return lax.rem(lax.broadcasted_iota(jnp.int32, (16, 128), 0), 4)


def lane_of():
    return lax.broadcasted_iota(jnp.int32, (16, 128), 1)


def column_pair(cells, lane):
    after = pltpu.roll(jnp.where(lane == 0, pltpu.roll(cells, 12, 0), cells), 127, 1)
    before = pltpu.roll(jnp.where(lane == 127, pltpu.roll(cells, 4, 0), cells), 1, 1)
    return after, before


def row_pair(cells, following, preceding, row):
    after = jnp.where(row == 3, pltpu.roll(following, 3, 0), pltpu.roll(cells, 15, 0))
    before = jnp.where(row == 0, pltpu.roll(preceding, 13, 0), pltpu.roll(cells, 1, 0))
    return after, before


def plane_pair(planes, p):
    zero = jnp.zeros_like(planes[0])
    after = planes[p + 1] if p + 1 < PLANES else zero
    before = planes[p - 1] if p > 0 else zero
    return after, before


def neighbours(core, mate, far):
    at_first = core == 0
    following = [jnp.where(at_first, m, f) for m, f in zip(mate, far)]
    preceding = [jnp.where(at_first, f, m) for m, f in zip(mate, far)]
    return following, preceding


def quad_sum(cells, row, lane):
    even_row = lax.rem(row, 2) == 0
    cells = cells + jnp.where(even_row, pltpu.roll(cells, 15, 0), pltpu.roll(cells, 1, 0))
    even_lane = lax.rem(lane, 2) == 0
    return cells + jnp.where(even_lane, pltpu.roll(cells, 127, 1), pltpu.roll(cells, 1, 1))


def spring_of(state):
    return 1.0 / (
        1.0
        - (state[0] * state[0] + state[1] * state[1] + state[2] * state[2]) * (1.0 / SPRING_LIMIT)
    )


def drift_of(state, kappa):
    half_spring = 0.5 * spring_of(state)
    return [
        kappa[a][0] * state[0] + kappa[a][1] * state[1] + kappa[a][2] * state[2]
        - half_spring * state[a]
        for a in range(3)
    ]


def capped(moved):
    length2 = moved[0] * moved[0] + moved[1] * moved[1] + moved[2] * moved[2]
    factor = jnp.minimum(1.0, RADIUS_CAP * lax.rsqrt(jnp.maximum(length2, RADIUS_CAP * RADIUS_CAP)))
    return [entry * factor for entry in moved]


def moments(state):
    spring = spring_of(state)
    scaled = [spring * state[a] for a in range(3)]
    return [scaled[a] * state[b] for a, b in PAIRS]


def advance_kernel(vel, mate, far, state, noise, moved, rim, rest):
    level = lax.axis_index("lvl")
    core = lax.rem(lax.axis_index("tile"), 2)
    row, lane = row_of(), lane_of()
    velocity = [[vel[a, p] for p in range(PLANES)] for a in range(3)]

    def gradient(p):
        result = []
        for a in range(3):
            following, preceding = neighbours(core, [mate[a, p]], [far[a, p]])
            pairs = (
                plane_pair(velocity[a], p),
                row_pair(velocity[a][p], following[0], preceding[0], row),
                column_pair(velocity[a][p], lane),
            )
            result.append([(after - before) * 0.5 for after, before in pairs])
        return result

    def emit(p, values):
        for i, c in enumerate(RIM):
            rim[i, p] = values[c]
        for i, c in enumerate(REST):
            rest[i, p] = values[c]

    @pl.when(level == 0)
    def _():
        for p in range(PLANES):
            kappa = gradient(p)

            def body(s, sums, p=p, kappa=kappa):
                q = [state[a, s, p] for a in range(3)]
                xi = [noise[0, a, s, p].astype(F32) + noise[1, a, s, p].astype(F32) for a in range(3)]
                drift = drift_of(q, kappa)
                out = capped([q[a] + STEP_TIME * drift[a] + NOISE_GAIN * xi[a] for a in range(3)])
                for a in range(3):
                    moved[a, s, p] = out[a]
                return tuple(t + m for t, m in zip(sums, moments(out)))

            sums = lax.fori_loop(0, SAMPLES, body, (jnp.zeros((16, 128), F32),) * 6, unroll=2)
            emit(p, [t * (1.0 / SAMPLES) - (1.0 if c < 3 else 0.0) for c, t in enumerate(sums)])

    @pl.when(level != 0)
    def _():
        for pair in range(PLANES // 2):
            first, second = gradient(2 * pair), gradient(2 * pair + 1)
            kappa = [
                [quad_sum(first[a][b] + second[a][b], row, lane) * 0.125 for b in range(3)]
                for a in range(3)
            ]

            def body(s, sums, pair=pair, kappa=kappa):
                for p in (2 * pair, 2 * pair + 1):
                    q = [state[a, s, p] for a in range(3)]
                    xa = [noise[0, a, s, p].astype(F32) for a in range(3)]
                    xb = [noise[1, a, s, p].astype(F32) for a in range(3)]
                    drift = drift_of(q, kappa)
                    coarse = capped(
                        [q[a] + STEP_TIME * drift[a] + NOISE_GAIN * (xa[a] + xb[a]) for a in range(3)]
                    )
                    half = capped(
                        [q[a] + (0.5 * STEP_TIME) * drift[a] + NOISE_GAIN * xa[a] for a in range(3)]
                    )
                    drift = drift_of(half, kappa)
                    fine = capped(
                        [half[a] + (0.5 * STEP_TIME) * drift[a] + NOISE_GAIN * xb[a] for a in range(3)]
                    )
                    for a in range(3):
                        moved[a, s, p] = fine[a]
                    sums = tuple(
                        t + (f - c) for t, f, c in zip(sums, moments(fine), moments(coarse))
                    )
                return sums

            sums = lax.fori_loop(0, SAMPLES, body, (jnp.zeros((16, 128), F32),) * 6)
            values = [quad_sum(t, row, lane) * (1.0 / 64.0) for t in sums]
            emit(2 * pair, values)
            emit(2 * pair + 1, values)


def join_kernel(own, other, total, toward_far, toward_mate):
    core = lax.rem(lax.axis_index("tile"), 2)
    total[...] = own[...] + other[...]
    far_row = core * 3
    for i in range(3):
        for p in range(PLANES):
            toward_far[i, p] = total[i, p, pl.ds(far_row, 4, stride=4), :]
            toward_mate[i, p] = total[i, p, pl.ds(3 - far_row, 4, stride=4), :]


def final_kernel(vel, mate, far, rim, rest, rest_other, rim_far, rim_mate, velocity_next, stress):
    core = lax.rem(lax.axis_index("tile"), 2)
    row, lane = row_of(), lane_of()
    for i, c in enumerate(RIM):
        stress[c] = rim[i]
    for i, c in enumerate(REST):
        stress[c] = rest[i] + rest_other[i]
    velocity = [[vel[a, p] for p in range(PLANES)] for a in range(3)]
    walls = [[stress[c, p] for p in range(PLANES)] for c in (0, 3, 4)]
    for p in range(PLANES):
        for a in range(3):
            following, preceding = neighbours(core, [mate[a, p]], [far[a, p]])
            own = velocity[a][p]
            pairs = (
                plane_pair(velocity[a], p),
                row_pair(own, following[0], preceding[0], row),
                column_pair(own, lane),
            )
            laplace = -6.0 * own
            carried = jnp.zeros_like(own)
            for b, (after, before) in enumerate(pairs):
                laplace = laplace + (after + before)
                carried = carried + velocity[b][p] * ((after - before) * 0.5)
            from_far = jnp.concatenate(
                [jnp.broadcast_to(rim_far[a, p, j : j + 1, :], (4, 128)) for j in range(4)], axis=0
            )
            from_mate = jnp.concatenate(
                [jnp.broadcast_to(rim_mate[a, p, j : j + 1, :], (4, 128)) for j in range(4)], axis=0
            )
            following, preceding = neighbours(core, [from_mate], [from_far])
            here = stress[RIM[a], p]
            y_after = jnp.where(row == 3, following[0], pltpu.roll(here, 15, 0))
            y_before = jnp.where(row == 0, preceding[0], pltpu.roll(here, 1, 0))
            x_after, x_before = plane_pair(walls[a], p)
            z_after, z_before = column_pair(stress[(4, 5, 2)[a], p], lane)
            force = (x_after - x_before) * 0.5 + (y_after - y_before) * 0.5 + (z_after - z_before) * 0.5
            velocity_next[a, p] = own + STEP_TIME * (
                VISCOSITY * laplace - carried + POLYMER_WEIGHT * force
            )


def shape(*extent):
    return jax.ShapeDtypeStruct(extent, F32)


def far_pairs(tiles):
    pairs = []
    for l in range(2):
        for t in range(1, tiles, 2):
            u = (t + 1) % tiles
            m = 1 - l if (t // 8) % 4 == 3 and t % 8 == 7 else l
            pairs += [(l * tiles + t, m * tiles + u), (m * tiles + u, l * tiles + t)]
    return pairs


def local(velocity, dumbbells, increments):
    tiles = lax.axis_size("tile")
    far_swap = far_pairs(tiles)
    mate_swap = [(t, t ^ 1) for t in range(tiles)]
    level_swap = [(0, 1), (1, 0)]
    vel = view(velocity)
    far = lax.ppermute(vel, ("lvl", "tile"), far_swap)
    mate = lax.ppermute(vel, "tile", mate_swap)
    moved, rim, rest = pl.pallas_call(
        advance_kernel,
        out_shape=[shape(3, SAMPLES, PLANES, 16, 128), shape(3, PLANES, 16, 128), shape(3, PLANES, 16, 128)],
    )(vel, mate, far, view(dumbbells[0]), view(increments[0]))
    rim_other = lax.ppermute(rim, "lvl", level_swap)
    rest_other = lax.ppermute(rest, "lvl", level_swap)
    rim_total, toward_far, toward_mate = pl.pallas_call(
        join_kernel,
        out_shape=[shape(3, PLANES, 16, 128), shape(3, PLANES, 4, 128), shape(3, PLANES, 4, 128)],
    )(rim, rim_other)
    rim_far = lax.ppermute(toward_far, ("lvl", "tile"), far_swap)
    rim_mate = lax.ppermute(toward_mate, "tile", mate_swap)
    velocity_next, stress = pl.pallas_call(
        final_kernel,
        out_shape=[shape(3, PLANES, 16, 128), shape(6, PLANES, 16, 128)],
    )(vel, mate, far, rim_total, rest, rest_other, rim_far, rim_mate)
    return (unview(velocity_next), unview(stress), unview(moved)[None])


def solution(mesh):
    in_specs = (
        P(None, None, "tile", None),
        P("lvl", None, None, None, "tile", None),
        P("lvl", None, None, None, None, "tile", None),
    )
    out_specs = (
        P(None, None, "tile", None),
        P(None, None, "tile", None),
        P("lvl", None, None, None, "tile", None),
    )
    return jax.shard_map(local, mesh=mesh, in_specs=in_specs, out_specs=out_specs, check_vma=False)
```

time: 190 us -> 42.2 us (0.22)
  waiting for transfers between devices: 99.6 us -> 13.2 us
  local copies, waits for them, and re-layouts: 50.3 us -> 1.91 us
  between operations: 14.3 us -> 0.65 us
  other arithmetic: 13.3 us -> 0 us
  Pallas kernels: 0 us -> 7.47 us
  starting transfers between devices: 11.5 us -> 18.7 us
    psum x1 -> x0, waiting for transfers between devices: 92.2 us -> none  [local(): stress = lax.psum(partial_value, 'lvl')]
    another operation x4 -> x0, local copies, waits for them, and re-layouts: 25.4 us -> none  [velocity_terms(): jnp.stack([(pairs[direction][0] - pairs[direction][1]) * 0.5 for directio...]
    mul x4 -> x0, local copies, waits for them, and re-layouts: 13.6 us -> none  [the longest x2 12.8 us: velocity_terms(): (pairs[direction][0] - pairs[direction][1]) * 0.5]
    slice x7 -> x0, local copies, waits for them, and re-layouts: 8.94 us -> none  [the longest x4 5.27 us: depth_pair(): return (jnp.roll(field, -1, axis=-1), jnp.roll(field, 1, axis=-1))]
    pallas_call x0 -> x3, Pallas kernels: none -> 7.47 us  [the longest x1 3.86 us: local(): pl.pallas_call(advance_kernel, out_shape=[shape(3, SAMPLES, PLANES, 16, 1...]
    ppermute x4 -> x6, starting transfers between devices: 11.5 us -> 18.7 us  [the longest x1 8.29 us: local(): far = lax.ppermute(vel, ('lvl', 'tile'), far_swap)]
    ppermute x4 -> x6, waiting for transfers between devices: 7.42 us -> 13.2 us  [the longest x1 6.33 us: local(): rim_other = lax.ppermute(rim, 'lvl', level_swap)]
    cond x5 -> x0, other arithmetic: 4.27 us -> none
  transfers between devices with their start and end apart: 5 -> 6, of which waited for: 2 -> 3; matrix products, arithmetic and copies ran while one was open for 11% -> 0% of each run, Pallas kernels for 0% -> 4%
where the time goes in v1:
time: 42.2 us; the launch traced here: 42 us
  starting transfers between devices  18.7 us (44%)
  waiting for transfers between devices  13.2 us (31%)
  Pallas kernels  7.47 us (18%)
  local copies, waits for them, and re-layouts  1.91 us (5%)
  between operations  0.65 us (2%)
    ppermute x1, starting transfers between devices, local(): far = lax.ppermute(vel, ('lvl', 'tile'), far_swap)  8.29 us
    ppermute x1, waiting for transfers between devices, local(): rim_other = lax.ppermute(rim, 'lvl', level_swap)  6.33 us
    ppermute x1, starting transfers between devices, local(): rim_other = lax.ppermute(rim, 'lvl', level_swap)  5.76 us
    ppermute x1, starting transfers between devices, local(): rim_far = lax.ppermute(toward_far, ('lvl', 'tile'), far_swap)  4.52 us
    ppermute x1, waiting for transfers between devices, local(): rim_far = lax.ppermute(toward_far, ('lvl', 'tile'), far_swap)  4.36 us
    pallas_call x1, Pallas kernels, local(): pl.pallas_call(advance_kernel, out_shape=[shape(3, SAMPLES, PLANES, 16, 1...  3.86 us
    ppermute x1, waiting for transfers between devices, local(): far = lax.ppermute(vel, ('lvl', 'tile'), far_swap)  2.53 us
    pallas_call x1, Pallas kernels, local(): pl.pallas_call(final_kernel, out_shape=[shape(3, PLANES, 16, 128), shape(...  2.01 us
  transfers between devices with their start and end apart: 6, of which 3 were waited for; matrix products, arithmetic and copies ran while one was open for 0% of the time, Pallas kernels for 4%

profile of v1, /device:TPU:0, one launch (start us, length us, event | category | flops | bytes accessed | tf_op | source)
XLA Modules:
  0.0 42.0 jit_solution(15363987374031240675)
XLA Ops:
  0.6 8.3 %collective-permute-start.1 = (f32[3,4,16,128]{3,2,1,0:T(8,128)}, f32[3,4,16,128]{3,2,1,0:T(8,128)S(1)}, u32[]{:S(2)}, u32[]{:S(2)}) collective-permute-start(f32[3,4,16,128]{3,2,1,0:T(8,128)} %bitcast.32), channel_id=1, source_target_pairs={{1,2},{2,1},{3,4},{4,3},{5,6},{6,5},{7,8},{8,7},{9,10},{10,9},{11,... | collective-permute-start | bytes 294920 | tf_op jit(solution)/shard_map/ppermute | solution.py:256
  8.9 0.0 collective-permute-start
  8.9 2.5 %collective-permute-done.1.far = f32[3,4,16,128]{3,2,1,0:T(8,128)S(1)} collective-permute-done((f32[3,4,16,128]{3,2,1,0:T(8,128)}, f32[3,4,16,128]{3,2,1,0:T(8,128)S(1)}, u32[]{:S(2)}, u32[]{:S(2)}) %collective-permute-start.1) | collective-permute-done | bytes 98336 | tf_op jit(solution)/shard_map/ppermute | solution.py:256
  11.5 0.0 copy-start
  11.5 0.0 collective-permute-done.mate
  11.5 0.0 copy-start.1
  11.5 0.6 %copy-done = f32[3,4,16,128]{3,2,1,0:T(8,128)} copy-done((f32[3,4,16,128]{3,2,1,0:T(8,128)}, f32[3,4,16,128]{3,2,1,0:T(8,128)S(1)}, u32[]{:S(2)}) %copy-start) | copy-done | bytes 98328
  12.1 0.0 copy-done.1
  12.1 3.9 %shard_map.58 = (f32[3,8,4,16,128]{4,3,2,1,0:T(8,128)}, f32[3,4,16,128]{3,2,1,0:T(8,128)}, f32[3,4,16,128]{3,2,1,0:T(8,128)}) custom-call(f32[3,4,16,128]{3,2,1,0:T(8,128)} %bitcast.34, f32[3,4,16,128]{3,2,1,0:T(8,128)} %copy-done.1, f32[3,4,16,128]{3,2,1,0:T(8,128)} %copy-done, f32[3,8,4,16,128]{4,3,2,1,0:T(8,128)} %bitcast.30, ...), custom_call_target="tpu_custom_call" | custom-call | tf_op jit(solution)/shard_map/pallas_call | solution.py:258
  16.0 5.8 %collective-permute-start.2 = (f32[3,4,16,128]{3,2,1,0:T(8,128)}, f32[3,4,16,128]{3,2,1,0:T(8,128)S(1)}, u32[]{:S(2)}, u32[]{:S(2)}) collective-permute-start(f32[3,4,16,128]{3,2,1,0:T(8,128)} %get-tuple-element.11.own), channel_id=1, source_target_pairs={{0,128},{128,0},{1,129},{129,1},{2,130},{130,2},{3,131},{131,3},{4... | collective-permute-start | bytes 294920 | tf_op jit(solution)/shard_map/ppermute | solution.py:262
  21.7 0.2 collective-permute-start.3
  21.9 6.3 %collective-permute-done.2.other = f32[3,4,16,128]{3,2,1,0:T(8,128)S(1)} collective-permute-done((f32[3,4,16,128]{3,2,1,0:T(8,128)}, f32[3,4,16,128]{3,2,1,0:T(8,128)S(1)}, u32[]{:S(2)}, u32[]{:S(2)}) %collective-permute-start.2) | collective-permute-done | bytes 98336 | tf_op jit(solution)/shard_map/ppermute | solution.py:262
  28.3 0.0 copy-start.3
  28.3 0.6 %copy-done.3 = f32[3,4,16,128]{3,2,1,0:T(8,128)} copy-done((f32[3,4,16,128]{3,2,1,0:T(8,128)}, f32[3,4,16,128]{3,2,1,0:T(8,128)S(1)}, u32[]{:S(2)}) %copy-start.3) | copy-done | bytes 98328
  28.9 1.6 %shard_map.59 = (f32[3,4,16,128]{3,2,1,0:T(8,128)}, f32[3,4,4,128]{3,2,1,0:T(4,128)}, f32[3,4,4,128]{3,2,1,0:T(4,128)}) custom-call(f32[3,4,16,128]{3,2,1,0:T(8,128)} %get-tuple-element.11.own, f32[3,4,16,128]{3,2,1,0:T(8,128)} %copy-done.3), custom_call_target="tpu_custom_call" | custom-call | tf_op jit(solution)/shard_map/pallas_call | solution.py:264
  30.5 4.5 %collective-permute-start.4 = (f32[3,4,4,128]{3,2,1,0:T(4,128)}, f32[3,4,4,128]{3,2,1,0:T(4,128)S(1)}, u32[]{:S(2)}, u32[]{:S(2)}) collective-permute-start(f32[3,4,4,128]{3,2,1,0:T(4,128)} %get-tuple-element.14), channel_id=1, source_target_pairs={{1,2},{2,1},{3,4},{4,3},{5,6},{6,5},{7,8},{8,7},{9,10},{10,9},{11,... | collective-permute-start | bytes 73736 | tf_op jit(solution)/shard_map/ppermute | solution.py:268
  35.0 0.0 collective-permute-start.5
  35.0 0.0 collective-permute-done.3.rest_other
  35.0 4.4 %collective-permute-done.4.rim_far = f32[3,4,4,128]{3,2,1,0:T(4,128)S(1)} collective-permute-done((f32[3,4,4,128]{3,2,1,0:T(4,128)}, f32[3,4,4,128]{3,2,1,0:T(4,128)S(1)}, u32[]{:S(2)}, u32[]{:S(2)}) %collective-permute-start.4) | collective-permute-done | bytes 24608 | tf_op jit(solution)/shard_map/ppermute | solution.py:268
  39.4 0.0 collective-permute-done.5.rim_mate
  39.4 0.0 copy-done.2
  39.4 0.6 %copy-done.4 = f32[3,4,4,128]{3,2,1,0:T(4,128)} copy-done((f32[3,4,4,128]{3,2,1,0:T(4,128)}, f32[3,4,4,128]{3,2,1,0:T(4,128)S(1)}, u32[]{:S(2)}) %copy-start.4) | copy-done | bytes 24600
  40.0 0.0 copy-done.5
  40.0 2.0 %shard_map.60 = (f32[3,4,16,128]{3,2,1,0:T(8,128)}, f32[6,4,16,128]{3,2,1,0:T(8,128)}) custom-call(f32[3,4,16,128]{3,2,1,0:T(8,128)} %bitcast.35, f32[3,4,16,128]{3,2,1,0:T(8,128)} %copy-done.1, f32[3,4,16,128]{3,2,1,0:T(8,128)} %copy-done, f32[3,4,16,128]{3,2,1,0:T(8,128)} %get-tuple-element.12.rim, f32[3,4,16,128]{3,2,1,0:T(8,128)} %get-tuple-element.13.rest, ...), custom_call_target="tpu_custom_call" | custom-call | tf_op jit(solution)/shard_map/pallas_call | solution.py:270
  (3 shorter events, 0.0 us)
Async XLA Ops:
  0.6 10.8 %collective-permute-start.1 = (f32[3,4,16,128]{3,2,1,0:T(8,128)}, f32[3,4,16,128]{3,2,1,0:T(8,128)S(1)}, u32[]{:S(2)}, u32[]{:S(2)}) collective-permute-start(f32[3,4,16,128]{3,2,1,0:T(8,128)} %bitcast.32), channel_id=1, source_target_pairs={{1,2},{2,1},{3,4},{4,3},{5,6},{6,5},{7,8},{8,7},{9,10},{10,9},{11,... | collective-permute-start | bytes 294920 | tf_op jit(solution)/shard_map/ppermute | solution.py:256
  8.9 2.5 %collective-permute-start = (f32[3,4,16,128]{3,2,1,0:T(8,128)}, f32[3,4,16,128]{3,2,1,0:T(8,128)S(1)}, u32[]{:S(2)}, u32[]{:S(2)}) collective-permute-start(f32[3,4,16,128]{3,2,1,0:T(8,128)} %bitcast.33), channel_id=1, source_target_pairs={{0,1},{1,0},{2,3},{3,2},{4,5},{5,4},{6,7},{7,6},{8,9},{9,8},{10,11... | collective-permute-start | bytes 294920 | tf_op jit(solution)/shard_map/ppermute | solution.py:257
  11.5 0.6 %copy-start = (f32[3,4,16,128]{3,2,1,0:T(8,128)}, f32[3,4,16,128]{3,2,1,0:T(8,128)S(1)}, u32[]{:S(2)}) copy-start(f32[3,4,16,128]{3,2,1,0:T(8,128)S(1)} %collective-permute-done.1.far) | copy-start | bytes 294916
  11.5 0.7 %copy-start.1 = (f32[3,4,16,128]{3,2,1,0:T(8,128)}, f32[3,4,16,128]{3,2,1,0:T(8,128)S(1)}, u32[]{:S(2)}) copy-start(f32[3,4,16,128]{3,2,1,0:T(8,128)S(1)} %collective-permute-done.mate) | copy-start | bytes 294916
  16.0 12.3 %collective-permute-start.2 = (f32[3,4,16,128]{3,2,1,0:T(8,128)}, f32[3,4,16,128]{3,2,1,0:T(8,128)S(1)}, u32[]{:S(2)}, u32[]{:S(2)}) collective-permute-start(f32[3,4,16,128]{3,2,1,0:T(8,128)} %get-tuple-element.11.own), channel_id=1, source_target_pairs={{0,128},{128,0},{1,129},{129,1},{2,130},{130,2},{3,131},{131,3},{4... | collective-permute-start | bytes 294920 | tf_op jit(solution)/shard_map/ppermute | solution.py:262
  21.7 13.3 %collective-permute-start.3 = (f32[3,4,16,128]{3,2,1,0:T(8,128)}, f32[3,4,16,128]{3,2,1,0:T(8,128)S(1)}, u32[]{:S(2)}, u32[]{:S(2)}) collective-permute-start(f32[3,4,16,128]{3,2,1,0:T(8,128)} %get-tuple-element.13.rest), channel_id=1, source_target_pairs={{0,128},{128,0},{1,129},{129,1},{2,130},{130,2},{3,131},{131,3},{4... | collective-permute-start | bytes 294920 | tf_op jit(solution)/shard_map/ppermute | solution.py:263
  28.3 0.6 %copy-start.3 = (f32[3,4,16,128]{3,2,1,0:T(8,128)}, f32[3,4,16,128]{3,2,1,0:T(8,128)S(1)}, u32[]{:S(2)}) copy-start(f32[3,4,16,128]{3,2,1,0:T(8,128)S(1)} %collective-permute-done.2.other) | copy-start | bytes 294916
  30.5 8.9 %collective-permute-start.4 = (f32[3,4,4,128]{3,2,1,0:T(4,128)}, f32[3,4,4,128]{3,2,1,0:T(4,128)S(1)}, u32[]{:S(2)}, u32[]{:S(2)}) collective-permute-start(f32[3,4,4,128]{3,2,1,0:T(4,128)} %get-tuple-element.14), channel_id=1, source_target_pairs={{1,2},{2,1},{3,4},{4,3},{5,6},{6,5},{7,8},{8,7},{9,10},{10,9},{11,... | collective-permute-start | bytes 73736 | tf_op jit(solution)/shard_map/ppermute | solution.py:268
  35.0 4.4 %collective-permute-start.5 = (f32[3,4,4,128]{3,2,1,0:T(4,128)}, f32[3,4,4,128]{3,2,1,0:T(4,128)S(1)}, u32[]{:S(2)}, u32[]{:S(2)}) collective-permute-start(f32[3,4,4,128]{3,2,1,0:T(4,128)} %get-tuple-element.15), channel_id=1, source_target_pairs={{0,1},{1,0},{2,3},{3,2},{4,5},{5,4},{6,7},{7,6},{8,9},{9,8},{10,11... | collective-permute-start | bytes 73736 | tf_op jit(solution)/shard_map/ppermute | solution.py:269
  35.0 4.4 %copy-start.2 = (f32[3,4,16,128]{3,2,1,0:T(8,128)}, f32[3,4,16,128]{3,2,1,0:T(8,128)S(1)}, u32[]{:S(2)}) copy-start(f32[3,4,16,128]{3,2,1,0:T(8,128)S(1)} %collective-permute-done.3.rest_other) | copy-start | bytes 294916
  39.4 0.6 %copy-start.4 = (f32[3,4,4,128]{3,2,1,0:T(4,128)}, f32[3,4,4,128]{3,2,1,0:T(4,128)S(1)}, u32[]{:S(2)}) copy-start(f32[3,4,4,128]{3,2,1,0:T(4,128)S(1)} %collective-permute-done.4.rim_far) | copy-start | bytes 73732
  39.4 0.6 %copy-start.5 = (f32[3,4,4,128]{3,2,1,0:T(4,128)}, f32[3,4,4,128]{3,2,1,0:T(4,128)S(1)}, u32[]{:S(2)}) copy-start(f32[3,4,4,128]{3,2,1,0:T(4,128)S(1)} %collective-permute-done.5.rim_mate) | copy-start | bytes 73732

commit v2 on v1

v2 whole, which is shorter than its diff:
```python
import functools
import math

import jax
import jax.numpy as jnp
from jax import lax
from jax.experimental import pallas as pl
from jax.experimental.pallas import tpu as pltpu
from jax.sharding import PartitionSpec as P

STEP_TIME = 0.25
SPRING_LIMIT = 10.0
RADIUS_CAP = 3.0
VISCOSITY = 0.5
POLYMER_WEIGHT = 0.2
NOISE_GAIN = math.sqrt(STEP_TIME / 2.0)
PLANES = 4
SAMPLES = 8
PAIRS = ((0, 0), (1, 1), (2, 2), (0, 1), (0, 2), (1, 2))
RIM = (3, 1, 5)
REST = (0, 2, 4)
F32 = jnp.float32
ANY = pl.BlockSpec(memory_space=pl.ANY)
VMEM = pl.BlockSpec(memory_space=pltpu.VMEM)


def view(field):
    lead = field.shape[:-2]
    split = field.reshape(lead + (4, 4, 128))
    return jnp.swapaxes(split, -3, -2).reshape(lead + (16, 128))


def unview(field):
    lead = field.shape[:-2]
    split = field.reshape(lead + (4, 4, 128))
    return jnp.swapaxes(split, -3, -2).reshape(lead + (4, 512))


def row_of():
    return lax.rem(lax.broadcasted_iota(jnp.int32, (16, 128), 0), 4)


def lane_of():
    return lax.broadcasted_iota(jnp.int32, (16, 128), 1)


def column_pair(cells, lane):
    after = pltpu.roll(jnp.where(lane == 0, pltpu.roll(cells, 12, 0), cells), 127, 1)
    before = pltpu.roll(jnp.where(lane == 127, pltpu.roll(cells, 4, 0), cells), 1, 1)
    return after, before


def row_pair(cells, following, preceding, row):
    after = jnp.where(row == 3, pltpu.roll(following, 3, 0), pltpu.roll(cells, 15, 0))
    before = jnp.where(row == 0, pltpu.roll(preceding, 13, 0), pltpu.roll(cells, 1, 0))
    return after, before


def plane_pair(planes, p):
    zero = jnp.zeros_like(planes[0])
    after = planes[p + 1] if p + 1 < PLANES else zero
    before = planes[p - 1] if p > 0 else zero
    return after, before


def neighbours(core, mate, far):
    at_first = core == 0
    following = [jnp.where(at_first, m, f) for m, f in zip(mate, far)]
    preceding = [jnp.where(at_first, f, m) for m, f in zip(mate, far)]
    return following, preceding


def quad_sum(cells, row, lane):
    even_row = lax.rem(row, 2) == 0
    cells = cells + jnp.where(even_row, pltpu.roll(cells, 15, 0), pltpu.roll(cells, 1, 0))
    even_lane = lax.rem(lane, 2) == 0
    return cells + jnp.where(even_lane, pltpu.roll(cells, 127, 1), pltpu.roll(cells, 1, 1))


def spring_of(state):
    return 1.0 / (
        1.0
        - (state[0] * state[0] + state[1] * state[1] + state[2] * state[2]) * (1.0 / SPRING_LIMIT)
    )


def applied(kappa, state):
    return [kappa[a][0] * state[0] + kappa[a][1] * state[1] + kappa[a][2] * state[2] for a in range(3)]


def capped(moved):
    length2 = moved[0] * moved[0] + moved[1] * moved[1] + moved[2] * moved[2]
    factor = jnp.minimum(1.0, RADIUS_CAP * lax.rsqrt(jnp.maximum(length2, RADIUS_CAP * RADIUS_CAP)))
    return [entry * factor for entry in moved]


def moments(state):
    spring = spring_of(state)
    scaled = [spring * state[a] for a in range(3)]
    return [scaled[a] * state[b] for a, b in PAIRS]


def prepare_kernel(state, noise, here, whole, first, later, bring, state_sem, noise_sem):
    level = lax.axis_index("lvl")

    def copies(s):
        return (
            pltpu.make_async_copy(state.at[:, s], here.at[:, s], state_sem.at[s]),
            pltpu.make_async_copy(noise.at[:, :, s], bring.at[:, :, s], noise_sem.at[s]),
        )

    for s in range(SAMPLES):
        for copy in copies(s):
            copy.start()

    def body(s, carry):
        for copy in copies(s):
            copy.wait()
        for p in range(PLANES):
            q = [here[a, s, p] for a in range(3)]
            xa = [NOISE_GAIN * bring[0, a, s, p].astype(F32) for a in range(3)]
            xb = [NOISE_GAIN * bring[1, a, s, p].astype(F32) for a in range(3)]
            spring = spring_of(q)
            keep = 1.0 - (0.5 * STEP_TIME) * spring
            for a in range(3):
                whole[a, s, p] = keep * q[a] + (xa[a] + xb[a])

            @pl.when(level != 0)
            def _():
                keep = 1.0 - (0.25 * STEP_TIME) * spring
                for a in range(3):
                    first[a, s, p] = keep * q[a] + xa[a]
                    later[a, s, p] = xb[a]

        return carry

    lax.fori_loop(0, SAMPLES, body, 0)


def advance_kernel(vel, mate, far, state, whole, first, later, moved, part, toward, rest):
    level = lax.axis_index("lvl")
    core = lax.rem(lax.axis_index("tile"), 2)
    row, lane = row_of(), lane_of()
    velocity = [[vel[a, p] for p in range(PLANES)] for a in range(3)]

    def gradient(p):
        result = []
        for a in range(3):
            following, preceding = neighbours(core, [mate[a, p]], [far[a, p]])
            pairs = (
                plane_pair(velocity[a], p),
                row_pair(velocity[a][p], following[0], preceding[0], row),
                column_pair(velocity[a][p], lane),
            )
            result.append([(after - before) * 0.5 for after, before in pairs])
        return result

    def emit(p, values):
        for c in range(6):
            part[c, p] = values[c]

    @pl.when(level == 0)
    def _():
        for p in range(PLANES):
            kappa = [[STEP_TIME * entry for entry in line] for line in gradient(p)]

            def body(s, sums, p=p, kappa=kappa):
                pull = applied(kappa, [state[a, s, p] for a in range(3)])
                out = capped([whole[a, s, p] + pull[a] for a in range(3)])
                for a in range(3):
                    moved[a, s, p] = out[a]
                return tuple(t + m for t, m in zip(sums, moments(out)))

            sums = lax.fori_loop(0, SAMPLES, body, (jnp.zeros((16, 128), F32),) * 6, unroll=2)
            emit(p, [t * (1.0 / SAMPLES) - (1.0 if c < 3 else 0.0) for c, t in enumerate(sums)])

    @pl.when(level != 0)
    def _():
        for pair in range(PLANES // 2):
            lower, upper = gradient(2 * pair), gradient(2 * pair + 1)
            kappa = [
                [quad_sum(lower[a][b] + upper[a][b], row, lane) * (0.125 * 0.5 * STEP_TIME) for b in range(3)]
                for a in range(3)
            ]

            def body(s, sums, pair=pair, kappa=kappa):
                for p in (2 * pair, 2 * pair + 1):
                    pull = applied(kappa, [state[a, s, p] for a in range(3)])
                    coarse = capped([whole[a, s, p] + 2.0 * pull[a] for a in range(3)])
                    half = capped([first[a, s, p] + pull[a] for a in range(3)])
                    pull = applied(kappa, half)
                    keep = 1.0 - (0.25 * STEP_TIME) * spring_of(half)
                    fine = capped([keep * half[a] + pull[a] + later[a, s, p] for a in range(3)])
                    for a in range(3):
                        moved[a, s, p] = fine[a]
                    sums = tuple(
                        t + (f - c) for t, f, c in zip(sums, moments(fine), moments(coarse))
                    )
                return sums

            sums = lax.fori_loop(0, SAMPLES, body, (jnp.zeros((16, 128), F32),) * 6)
            values = [quad_sum(t, row, lane) * (1.0 / 64.0) for t in sums]
            emit(2 * pair, values)
            emit(2 * pair + 1, values)

    far_row = core * 3
    for i, c in enumerate(RIM):
        for p in range(PLANES):
            toward[0, i, p] = part[c, p, pl.ds(far_row, 4, stride=4), :]
            toward[1, i, p] = part[c, p, pl.ds(3 - far_row, 4, stride=4), :]
            rest[i, p, 16:20] = part[c, p, pl.ds(1, 4, stride=4), :]
            rest[i, p, 20:24] = part[c, p, pl.ds(2, 4, stride=4), :]
    for i, c in enumerate(REST):
        for p in range(PLANES):
            rest[i, p, 0:16] = part[c, p]


def momentum_kernel(vel, mate, far, moved, solvent, stored, sem):
    copy = pltpu.make_async_copy(moved, stored, sem)
    copy.start()
    core = lax.rem(lax.axis_index("tile"), 2)
    row, lane = row_of(), lane_of()
    velocity = [[vel[a, p] for p in range(PLANES)] for a in range(3)]
    for p in range(PLANES):
        for a in range(3):
            following, preceding = neighbours(core, [mate[a, p]], [far[a, p]])
            here = velocity[a][p]
            pairs = (
                plane_pair(velocity[a], p),
                row_pair(here, following[0], preceding[0], row),
                column_pair(here, lane),
            )
            laplace = -6.0 * here
            carried = jnp.zeros_like(here)
            for b, (after, before) in enumerate(pairs):
                laplace = laplace + (after + before)
                carried = carried + velocity[b][p] * ((after - before) * 0.5)
            solvent[a, p] = here + STEP_TIME * (VISCOSITY * laplace - carried)
    copy.wait()


def over_runs(rows):
    return jnp.concatenate([jnp.broadcast_to(rows[j : j + 1], (4, 128)) for j in range(4)], axis=0)


def final_kernel(solvent, part, rest, edges, from_far, from_mate, velocity_next, stress):
    core = lax.rem(lax.axis_index("tile"), 2)
    row, lane = row_of(), lane_of()
    far_row = core * 3
    for i, c in enumerate(RIM):
        for p in range(PLANES):
            stress[c, p, pl.ds(far_row, 4, stride=4), :] = edges[0, i, p]
            stress[c, p, pl.ds(3 - far_row, 4, stride=4), :] = edges[1, i, p]
            for r in (1, 2):
                own = part[c, p, pl.ds(r, 4, stride=4), :]
                stress[c, p, pl.ds(r, 4, stride=4), :] = own + rest[i, p, 12 + 4 * r : 16 + 4 * r]
    for i, c in enumerate(REST):
        for p in range(PLANES):
            stress[c, p] = part[c, p] + rest[i, p, 0:16]
    walls = [[stress[c, p] for p in range(PLANES)] for c in (0, 3, 4)]
    for p in range(PLANES):
        for a in range(3):
            following, preceding = neighbours(core, [over_runs(from_mate[a, p])], [over_runs(from_far[a, p])])
            rim = stress[RIM[a], p]
            y_after = jnp.where(row == 3, following[0], pltpu.roll(rim, 15, 0))
            y_before = jnp.where(row == 0, preceding[0], pltpu.roll(rim, 1, 0))
            x_after, x_before = plane_pair(walls[a], p)
            z_after, z_before = column_pair(stress[(4, 5, 2)[a], p], lane)
            force = (x_after - x_before) * 0.5 + (y_after - y_before) * 0.5 + (z_after - z_before) * 0.5
            velocity_next[a, p] = solvent[a, p] + (STEP_TIME * POLYMER_WEIGHT) * force


def limit(mebibytes):
    return pltpu.CompilerParams(vmem_limit_bytes=mebibytes * 2**20)


def shape(*extent):
    return jax.ShapeDtypeStruct(extent, F32)


def far_pairs(tiles):
    pairs = []
    for l in range(2):
        for t in range(1, tiles, 2):
            u = (t + 1) % tiles
            m = 1 - l if (t // 8) % 4 == 3 and t % 8 == 7 else l
            pairs += [(l * tiles + t, m * tiles + u), (m * tiles + u, l * tiles + t)]
    return pairs


def local(velocity, dumbbells, increments):
    tiles = lax.axis_size("tile")
    far_swap = far_pairs(tiles)
    mate_swap = [(t, t ^ 1) for t in range(tiles)]
    level_swap = [(0, 1), (1, 0)]
    vel = view(velocity)
    far = lax.ppermute(vel, ("lvl", "tile"), far_swap)
    mate = lax.ppermute(vel, "tile", mate_swap)
    field = (3, PLANES, 16, 128)
    ensemble = (3, SAMPLES, PLANES, 16, 128)
    here, whole, first, later = pl.pallas_call(
        prepare_kernel,
        out_shape=[shape(*ensemble)] * 4,
        in_specs=[ANY] * 2,
        out_specs=[VMEM] * 4,
        scratch_shapes=[
            pltpu.VMEM((2,) + ensemble, jnp.bfloat16),
            pltpu.SemaphoreType.DMA((SAMPLES,)),
            pltpu.SemaphoreType.DMA((SAMPLES,)),
        ],
        compiler_params=limit(16),
    )(view(dumbbells[0]), view(increments[0]))
    moved, part, toward, rest = pl.pallas_call(
        advance_kernel,
        out_shape=[shape(*ensemble), shape(6, PLANES, 16, 128), shape(2, 3, PLANES, 4, 128), shape(3, PLANES, 24, 128)],
        in_specs=[VMEM] * 7,
        out_specs=[VMEM] * 4,
        compiler_params=limit(16),
    )(vel, mate, far, here, whole, first, later)
    toward_other = lax.ppermute(toward, "lvl", level_swap)
    rest_other = lax.ppermute(rest, "lvl", level_swap)
    edges = toward + toward_other
    from_far = lax.ppermute(edges[0], ("lvl", "tile"), far_swap)
    from_mate = lax.ppermute(edges[1], "tile", mate_swap)
    solvent, stored = pl.pallas_call(
        momentum_kernel,
        out_shape=[shape(*field), shape(*ensemble)],
        in_specs=[VMEM] * 3 + [ANY],
        out_specs=[VMEM, ANY],
        scratch_shapes=[pltpu.SemaphoreType.DMA],
        compiler_params=limit(8),
    )(vel, mate, far, moved)
    velocity_next, stress = pl.pallas_call(
        final_kernel,
        out_shape=[shape(*field), shape(6, PLANES, 16, 128)],
        in_specs=[VMEM] * 6,
        out_specs=[VMEM] * 2,
        compiler_params=limit(8),
    )(solvent, part, rest_other, edges, from_far, from_mate)
    return (unview(velocity_next), unview(stress), unview(stored)[None])


def solution(mesh):
    in_specs = (
        P(None, None, "tile", None),
        P("lvl", None, None, None, "tile", None),
        P("lvl", None, None, None, None, "tile", None),
    )
    out_specs = (
        P(None, None, "tile", None),
        P(None, None, "tile", None),
        P("lvl", None, None, None, "tile", None),
    )
    return jax.shard_map(local, mesh=mesh, in_specs=in_specs, out_specs=out_specs, check_vma=False)
```

time: 42.2 us -> 35.7 us (0.85)
  Pallas kernels: 7.47 us -> 4.06 us
  waiting for transfers between devices: 13.2 us -> 11 us
  starting transfers between devices: 18.7 us -> 17.4 us
    pallas_call x3 -> x4, Pallas kernels: 7.47 us -> 4.06 us  [the longest x1 1.24 us: local(): pl.pallas_call(prepare_kernel, out_shape=[shape(*ensemble)] * 4, in_specs...]
    ppermute x3, starting transfers between devices: 10.3 us -> 7.74 us  [the longest x1 4.61 us: local(): toward_other = lax.ppermute(toward, 'lvl', level_swap)]
    ppermute x1, waiting for transfers between devices: 2.53 us -> 0.01 us  [local(): far = lax.ppermute(vel, ('lvl', 'tile'), far_swap)]
    ppermute x1, starting transfers between devices: 0.17 us -> 1.41 us  [local(): rest_other = lax.ppermute(rest, 'lvl', level_swap)]
    unnamed x12 -> x6, local copies, waits for them, and re-layouts: 1.91 us -> 2.27 us
  transfers between devices with their start and end apart: 6 -> 6, of which waited for: 3 -> 2; matrix products, arithmetic and copies ran while one was open for 0% -> 0% of each run, Pallas kernels for 4% -> 6%
where the time goes in v2:
time: 35.7 us; the launch traced here: 35.5 us
  starting transfers between devices  17.4 us (49%)
  waiting for transfers between devices  11 us (31%)
  Pallas kernels  4.06 us (11%)
  local copies, waits for them, and re-layouts  2.28 us (6%)
  between operations  0.7 us (2%)
    ppermute x1, starting transfers between devices, local(): far = lax.ppermute(vel, ('lvl', 'tile'), far_swap)  8.29 us
    ppermute x1, waiting for transfers between devices, local(): toward_other = lax.ppermute(toward, 'lvl', level_swap)  6.17 us
    ppermute x1, waiting for transfers between devices, local(): from_far = lax.ppermute(edges[0], ('lvl', 'tile'), far_swap)  4.83 us
    ppermute x1, starting transfers between devices, local(): toward_other = lax.ppermute(toward, 'lvl', level_swap)  4.61 us
    ppermute x1, starting transfers between devices, local(): from_far = lax.ppermute(edges[0], ('lvl', 'tile'), far_swap)  3.02 us
    unnamed x6, local copies, waits for them, and re-layouts  2.27 us
    ppermute x1, starting transfers between devices, local(): rest_other = lax.ppermute(rest, 'lvl', level_swap)  1.41 us
    pallas_call x1, Pallas kernels, local(): pl.pallas_call(prepare_kernel, out_shape=[shape(*ensemble)] * 4, in_specs...  1.24 us
  transfers between devices with their start and end apart: 6, of which 2 were waited for; matrix products, arithmetic and copies ran while one was open for 0% of the time, Pallas kernels for 6%

profile of v2, /device:TPU:0, one launch (start us, length us, event | category | flops | bytes accessed | tf_op | source)
XLA Modules:
  0.0 35.5 jit_solution(3505863395633151214)
XLA Ops:
  0.6 8.3 %collective-permute-start.1 = (f32[3,4,16,128]{3,2,1,0:T(8,128)}, f32[3,4,16,128]{3,2,1,0:T(8,128)S(1)}, u32[]{:S(2)}, u32[]{:S(2)}) collective-permute-start(f32[3,4,16,128]{3,2,1,0:T(8,128)} %bitcast.36), channel_id=1, source_target_pairs={{1,2},{2,1},{3,4},{4,3},{5,6},{6,5},{7,8},{8,7},{9,10},{10,9},{11,... | collective-permute-start | bytes 294920 | tf_op jit(solution)/shard_map/ppermute | solution.py:297
  8.9 0.0 collective-permute-start
  8.9 0.0 copy-start
  8.9 1.1 %copy-done = f32[1,3,8,4,4,512]{5,4,3,2,1,0:T(4,128)S(1)} copy-done((f32[1,3,8,4,4,512]{5,4,3,2,1,0:T(4,128)S(1)}, f32[1,3,8,4,4,512]{5,4,3,2,1,0:T(4,128)}, u32[]{:S(2)}) %copy-start) | copy-done | bytes 786456
  10.1 0.0 copy-start.1
  10.1 1.1 %copy-done.1 = bf16[1,2,3,8,4,4,512]{6,5,4,3,2,1,0:T(4,128)(2,1)S(1)} copy-done((bf16[1,2,3,8,4,4,512]{6,5,4,3,2,1,0:T(4,128)(2,1)S(1)}, bf16[1,2,3,8,4,4,512]{6,5,4,3,2,1,0:T(4,128)(2,1)}, u32[]{:S(2)}) %copy-start.1) | copy-done | bytes 786456
  11.2 0.0 copy-start.2
  11.2 1.2 %shard_map.58 = (f32[3,8,4,16,128]{4,3,2,1,0:T(8,128)S(1)}, f32[3,8,4,16,128]{4,3,2,1,0:T(8,128)S(1)}, f32[3,8,4,16,128]{4,3,2,1,0:T(8,128)S(1)}, f32[3,8,4,16,128]{4,3,2,1,0:T(8,128)S(1)}) custom-call(f32[3,8,4,16,128]{4,3,2,1,0:T(8,128)S(1)} %bitcast.34, bf16[2,3,8,4,16,128]{5,4,3,2,1,0:T(8,128)(2,1)S(1)} %bitcast.35), custom_call_target="tpu_custom_call" | custom-call | tf_op jit(solution)/shard_map/pallas_call | solution.py:301
  12.4 0.0 collective-permute-done.1.far
  12.5 0.0 collective-permute-done.mate
  12.5 0.0 copy-done.2
  12.5 1.1 %shard_map.59 = (f32[3,8,4,16,128]{4,3,2,1,0:T(8,128)S(1)}, f32[6,4,16,128]{3,2,1,0:T(8,128)S(1)}, f32[2,3,4,4,128]{4,3,2,1,0:T(4,128)S(1)}, f32[3,4,24,128]{3,2,1,0:T(8,128)S(1)}) custom-call(f32[3,4,16,128]{3,2,1,0:T(8,128)S(1)} %bitcast.38, f32[3,4,16,128]{3,2,1,0:T(8,128)S(1)} %collective-permute-done.mate, ...), custom_call_target="tpu_custom_call" | custom-call | tf_op jit(solution)/shard_map/pallas_call | solution.py:313
  13.6 4.6 %collective-permute-start.3 = (f32[2,3,4,4,128]{4,3,2,1,0:T(4,128)S(1)}, f32[2,3,4,4,128]{4,3,2,1,0:T(4,128)S(1)}, u32[]{:S(2)}, u32[]{:S(2)}) collective-permute-start(f32[2,3,4,4,128]{4,3,2,1,0:T(4,128)S(1)} %get-tuple-element.23), channel_id=1, source_target_pairs={{0,128},{128,0},{1,129},{129,1},{2,130},{130,2},{3,131},{131,3},{4... | collective-permute-start | bytes 147464 | tf_op jit(solution)/shard_map/ppermute | solution.py:320
  18.2 1.4 %collective-permute-start.2 = (f32[3,4,24,128]{3,2,1,0:T(8,128)S(1)}, f32[3,4,24,128]{3,2,1,0:T(8,128)S(1)}, u32[]{:S(2)}, u32[]{:S(2)}) collective-permute-start(f32[3,4,24,128]{3,2,1,0:T(8,128)S(1)} %get-tuple-element.22), channel_id=1, source_target_pairs={{0,128},{128,0},{1,129},{129,1},{2,130},{130,2},{3,131},{131,3},{4... | collective-permute-start | bytes 442376 | tf_op jit(solution)/shard_map/ppermute | solution.py:321
  19.6 6.2 %collective-permute-done.3 = f32[2,3,4,4,128]{4,3,2,1,0:T(4,128)S(1)} collective-permute-done((f32[2,3,4,4,128]{4,3,2,1,0:T(4,128)S(1)}, f32[2,3,4,4,128]{4,3,2,1,0:T(4,128)S(1)}, u32[]{:S(2)}, u32[]{:S(2)}) %collective-permute-start.3) | collective-permute-done | bytes 49184 | tf_op jit(solution)/shard_map/ppermute | solution.py:320
  25.8 0.1 collective-permute-start.5
  26.0 3.0 %collective-permute-start.4 = (f32[3,4,4,128]{3,2,1,0:T(4,128)S(1)}, f32[3,4,4,128]{3,2,1,0:T(4,128)S(1)}, u32[]{:S(2)}, u32[]{:S(2)}) collective-permute-start(f32[3,4,4,128]{3,2,1,0:T(4,128)S(1)} %get-tuple-element.28), channel_id=1, source_target_pairs={{1,2},{2,1},{3,4},{4,3},{5,6},{6,5},{7,8},{8,7},{9,10},{10,9},{11,... | collective-permute-start | bytes 73736 | tf_op jit(solution)/shard_map/ppermute | solution.py:323
  29.0 0.9 %shard_map.60 = (f32[3,4,16,128]{3,2,1,0:T(8,128)S(1)}, f32[3,8,4,16,128]{4,3,2,1,0:T(8,128)}) custom-call(f32[3,4,16,128]{3,2,1,0:T(8,128)S(1)} %bitcast.39, f32[3,4,16,128]{3,2,1,0:T(8,128)S(1)} %collective-permute-done.mate, f32[3,4,16,128]{3,2,1,0:T(8,128)S(1)} %collective-permute-done.1.far, f32[3,8,4,16,128]{4,3,2,1,0:T(8,128)S(1)} %get-tuple-element.19.moved), custom_call_target="tpu_custom_call" | custom-call | tf_op jit(solution)/shard_map/pallas_call | solution.py:325
  29.9 0.0 collective-permute-done.5.from_mate
  29.9 4.8 %collective-permute-done.4.from_far = f32[3,4,4,128]{3,2,1,0:T(4,128)S(1)} collective-permute-done((f32[3,4,4,128]{3,2,1,0:T(4,128)S(1)}, f32[3,4,4,128]{3,2,1,0:T(4,128)S(1)}, u32[]{:S(2)}, u32[]{:S(2)}) %collective-permute-start.4) | collective-permute-done | bytes 24608 | tf_op jit(solution)/shard_map/ppermute | solution.py:323
  34.7 0.0 collective-permute-done.2.rest
  34.7 0.8 %shard_map.61 = (f32[3,4,16,128]{3,2,1,0:T(8,128)}, f32[6,4,16,128]{3,2,1,0:T(8,128)}) custom-call(f32[3,4,16,128]{3,2,1,0:T(8,128)S(1)} %get-tuple-element.20.solvent, f32[6,4,16,128]{3,2,1,0:T(8,128)S(1)} %get-tuple-element.21.part, f32[3,4,24,128]{3,2,1,0:T(8,128)S(1)} %collective-permute-done.2.rest, f32[2,3,4,4,128]{4,3,2,1,0:T(4,128)S(1)} %add.3.edges, ...), custom_call_target="tpu_custom_call" | custom-call | tf_op jit(solution)/shard_map/pallas_call | solution.py:333
  (2 shorter events, 0.0 us)
Async XLA Ops:
  0.6 11.8 %collective-permute-start.1 = (f32[3,4,16,128]{3,2,1,0:T(8,128)}, f32[3,4,16,128]{3,2,1,0:T(8,128)S(1)}, u32[]{:S(2)}, u32[]{:S(2)}) collective-permute-start(f32[3,4,16,128]{3,2,1,0:T(8,128)} %bitcast.36), channel_id=1, source_target_pairs={{1,2},{2,1},{3,4},{4,3},{5,6},{6,5},{7,8},{8,7},{9,10},{10,9},{11,... | collective-permute-start | bytes 294920 | tf_op jit(solution)/shard_map/ppermute | solution.py:297
  8.9 3.5 %collective-permute-start = (f32[3,4,16,128]{3,2,1,0:T(8,128)}, f32[3,4,16,128]{3,2,1,0:T(8,128)S(1)}, u32[]{:S(2)}, u32[]{:S(2)}) collective-permute-start(f32[3,4,16,128]{3,2,1,0:T(8,128)} %bitcast.37), channel_id=1, source_target_pairs={{0,1},{1,0},{2,3},{3,2},{4,5},{5,4},{6,7},{7,6},{8,9},{9,8},{10,11... | collective-permute-start | bytes 294920 | tf_op jit(solution)/shard_map/ppermute | solution.py:298
  8.9 1.1 %copy-start = (f32[1,3,8,4,4,512]{5,4,3,2,1,0:T(4,128)S(1)}, f32[1,3,8,4,4,512]{5,4,3,2,1,0:T(4,128)}, u32[]{:S(2)}) copy-start(f32[1,3,8,4,4,512]{5,4,3,2,1,0:T(4,128)} %param.4) | copy-start | bytes 2359300
  10.1 1.1 %copy-start.1 = (bf16[1,2,3,8,4,4,512]{6,5,4,3,2,1,0:T(4,128)(2,1)S(1)}, bf16[1,2,3,8,4,4,512]{6,5,4,3,2,1,0:T(4,128)(2,1)}, u32[]{:S(2)}) copy-start(bf16[1,2,3,8,4,4,512]{6,5,4,3,2,1,0:T(4,128)(2,1)} %param.5) | copy-start | bytes 2359300
  11.2 1.3 %copy-start.2 = (f32[3,4,4,512]{3,2,1,0:T(4,128)S(1)}, f32[3,4,4,512]{3,2,1,0:T(4,128)}, u32[]{:S(2)}) copy-start(f32[3,4,4,512]{3,2,1,0:T(4,128)} %param.3) | copy-start | bytes 294916
  13.6 12.2 %collective-permute-start.3 = (f32[2,3,4,4,128]{4,3,2,1,0:T(4,128)S(1)}, f32[2,3,4,4,128]{4,3,2,1,0:T(4,128)S(1)}, u32[]{:S(2)}, u32[]{:S(2)}) collective-permute-start(f32[2,3,4,4,128]{4,3,2,1,0:T(4,128)S(1)} %get-tuple-element.23), channel_id=1, source_target_pairs={{0,128},{128,0},{1,129},{129,1},{2,130},{130,2},{3,131},{131,3},{4... | collective-permute-start | bytes 147464 | tf_op jit(solution)/shard_map/ppermute | solution.py:320
  18.2 16.5 %collective-permute-start.2 = (f32[3,4,24,128]{3,2,1,0:T(8,128)S(1)}, f32[3,4,24,128]{3,2,1,0:T(8,128)S(1)}, u32[]{:S(2)}, u32[]{:S(2)}) collective-permute-start(f32[3,4,24,128]{3,2,1,0:T(8,128)S(1)} %get-tuple-element.22), channel_id=1, source_target_pairs={{0,128},{128,0},{1,129},{129,1},{2,130},{130,2},{3,131},{131,3},{4... | collective-permute-start | bytes 442376 | tf_op jit(solution)/shard_map/ppermute | solution.py:321
  25.8 4.0 %collective-permute-start.5 = (f32[3,4,4,128]{3,2,1,0:T(4,128)S(1)}, f32[3,4,4,128]{3,2,1,0:T(4,128)S(1)}, u32[]{:S(2)}, u32[]{:S(2)}) collective-permute-start(f32[3,4,4,128]{3,2,1,0:T(4,128)S(1)} %get-tuple-element.27), channel_id=1, source_target_pairs={{0,1},{1,0},{2,3},{3,2},{4,5},{5,4},{6,7},{7,6},{8,9},{9,8},{10,11... | collective-permute-start | bytes 73736 | tf_op jit(solution)/shard_map/ppermute | solution.py:324
  26.0 8.8 %collective-permute-start.4 = (f32[3,4,4,128]{3,2,1,0:T(4,128)S(1)}, f32[3,4,4,128]{3,2,1,0:T(4,128)S(1)}, u32[]{:S(2)}, u32[]{:S(2)}) collective-permute-start(f32[3,4,4,128]{3,2,1,0:T(4,128)S(1)} %get-tuple-element.28), channel_id=1, source_target_pairs={{1,2},{2,1},{3,4},{4,3},{5,6},{6,5},{7,8},{8,7},{9,10},{10,9},{11,... | collective-permute-start | bytes 73736 | tf_op jit(solution)/shard_map/ppermute | solution.py:323

commit v3 on v2

--- a/solution.py
+++ b/solution.py
@@ -50,9 +50,10 @@
     return after, before
 
 
-def row_pair(cells, following, preceding, row):
-    after = jnp.where(row == 3, pltpu.roll(following, 3, 0), pltpu.roll(cells, 15, 0))
-    before = jnp.where(row == 0, pltpu.roll(preceding, 13, 0), pltpu.roll(cells, 1, 0))
+def row_pair(cells, edges, row):
+    following, preceding = edges
+    after = jnp.where(row == 3, following, pltpu.roll(cells, 15, 0))
+    before = jnp.where(row == 0, preceding, pltpu.roll(cells, 1, 0))
     return after, before
 
 
@@ -63,11 +64,20 @@
     return after, before
 
 
-def neighbours(core, mate, far):
-    at_first = core == 0
-    following = [jnp.where(at_first, m, f) for m, f in zip(mate, far)]
-    preceding = [jnp.where(at_first, f, m) for m, f in zip(mate, far)]
+def over_runs(rows):
+    return jnp.concatenate([jnp.broadcast_to(rows[j : j + 1], (4, 128)) for j in range(4)], axis=0)
+
+
+def block_edges(core, mate, far):
+    rows = over_runs(far)
+    following = jnp.where(core == 0, pltpu.roll(mate, 3, 0), rows)
+    preceding = jnp.where(core == 0, rows, pltpu.roll(mate, 13, 0))
     return following, preceding
+
+
+def row_edges(core, mate, far):
+    mate, far = over_runs(mate), over_runs(far)
+    return jnp.where(core == 0, mate, far), jnp.where(core == 0, far, mate)
 
 
 def quad_sum(cells, row, lane):
@@ -78,10 +88,10 @@
 
 
 def spring_of(state):
-    return 1.0 / (
-        1.0
-        - (state[0] * state[0] + state[1] * state[1] + state[2] * state[2]) * (1.0 / SPRING_LIMIT)
-    )
+    length2 = state[0] * state[0] + state[1] * state[1] + state[2] * state[2]
+    slack = 1.0 - length2 * (1.0 / SPRING_LIMIT)
+    guess = pl.reciprocal(slack, approx=True)
+    return guess * (2.0 - slack * guess)
 
 
 def applied(kappa, state):
@@ -98,6 +108,13 @@
     spring = spring_of(state)
     scaled = [spring * state[a] for a in range(3)]
     return [scaled[a] * state[b] for a, b in PAIRS]
+
+
+def edge_kernel(vel, toward_far):
+    far_row = 3 * lax.rem(lax.axis_index("tile"), 2)
+    for a in range(3):
+        for p in range(PLANES):
+            toward_far[a, p] = vel[a, p, pl.ds(far_row, 4, stride=4), :]
 
 
 def prepare_kernel(state, noise, here, whole, first, later, bring, state_sem, noise_sem):
@@ -137,7 +154,7 @@
     lax.fori_loop(0, SAMPLES, body, 0)
 
 
-def advance_kernel(vel, mate, far, state, whole, first, later, moved, part, toward, rest):
+def advance_kernel(vel, mate, far, state, whole, first, later, moved, part, toward, packed):
     level = lax.axis_index("lvl")
     core = lax.rem(lax.axis_index("tile"), 2)
     row, lane = row_of(), lane_of()
@@ -146,10 +163,9 @@
     def gradient(p):
         result = []
         for a in range(3):
-            following, preceding = neighbours(core, [mate[a, p]], [far[a, p]])
             pairs = (
                 plane_pair(velocity[a], p),
-                row_pair(velocity[a][p], following[0], preceding[0], row),
+                row_pair(velocity[a][p], block_edges(core, mate[a, p], far[a, p]), row),
                 column_pair(velocity[a][p], lane),
             )
             result.append([(after - before) * 0.5 for after, before in pairs])
@@ -208,26 +224,42 @@
         for p in range(PLANES):
             toward[0, i, p] = part[c, p, pl.ds(far_row, 4, stride=4), :]
             toward[1, i, p] = part[c, p, pl.ds(3 - far_row, 4, stride=4), :]
-            rest[i, p, 16:20] = part[c, p, pl.ds(1, 4, stride=4), :]
-            rest[i, p, 20:24] = part[c, p, pl.ds(2, 4, stride=4), :]
+
+    for e in range(2):
+        for i in range(3):
+            for p in range(PLANES):
+                packed[(e * 3 + i) * PLANES + p] = toward[e, i, p]
+
+    @pl.when(level == 0)
+    def _():
+        for i, c in enumerate(RIM):
+            for p in range(PLANES):
+                for r in (1, 2):
+                    packed[23 + (i * PLANES + p) * 2 + r] = part[c, p, pl.ds(r, 4, stride=4), :]
+
+    @pl.when(level != 0)
+    def _():
+        for g in range(2):
+            for c in range(6):
+                for pair in range(PLANES // 2):
+                    packed[24 + (g * 6 + c) * 2 + pair] = part[c, 2 * pair, pl.ds(2 * g, 4, stride=4), :]
+
+
+def momentum_kernel(vel, mate, far, moved, part, solvent, stored, rest, sem):
+    copy = pltpu.make_async_copy(moved, stored, sem)
+    copy.start()
     for i, c in enumerate(REST):
         for p in range(PLANES):
-            rest[i, p, 0:16] = part[c, p]
-
-
-def momentum_kernel(vel, mate, far, moved, solvent, stored, sem):
-    copy = pltpu.make_async_copy(moved, stored, sem)
-    copy.start()
+            rest[i, p] = part[c, p]
     core = lax.rem(lax.axis_index("tile"), 2)
     row, lane = row_of(), lane_of()
     velocity = [[vel[a, p] for p in range(PLANES)] for a in range(3)]
     for p in range(PLANES):
         for a in range(3):
-            following, preceding = neighbours(core, [mate[a, p]], [far[a, p]])
             here = velocity[a][p]
             pairs = (
                 plane_pair(velocity[a], p),
-                row_pair(here, following[0], preceding[0], row),
+                row_pair(here, block_edges(core, mate[a, p], far[a, p]), row),
                 column_pair(here, lane),
             )
             laplace = -6.0 * here
@@ -239,31 +271,40 @@
     copy.wait()
 
 
-def over_runs(rows):
-    return jnp.concatenate([jnp.broadcast_to(rows[j : j + 1], (4, 128)) for j in range(4)], axis=0)
-
-
-def final_kernel(solvent, part, rest, edges, from_far, from_mate, velocity_next, stress):
+def final_kernel(solvent, part, packed, rest, edges, from_far, from_mate, velocity_next, stress):
+    level = lax.axis_index("lvl")
     core = lax.rem(lax.axis_index("tile"), 2)
     row, lane = row_of(), lane_of()
     far_row = core * 3
-    for i, c in enumerate(RIM):
-        for p in range(PLANES):
-            stress[c, p, pl.ds(far_row, 4, stride=4), :] = edges[0, i, p]
-            stress[c, p, pl.ds(3 - far_row, 4, stride=4), :] = edges[1, i, p]
-            for r in (1, 2):
-                own = part[c, p, pl.ds(r, 4, stride=4), :]
-                stress[c, p, pl.ds(r, 4, stride=4), :] = own + rest[i, p, 12 + 4 * r : 16 + 4 * r]
-    for i, c in enumerate(REST):
-        for p in range(PLANES):
-            stress[c, p] = part[c, p] + rest[i, p, 0:16]
+
+    @pl.when(level == 0)
+    def _():
+        for c in range(6):
+            for pair in range(PLANES // 2):
+                place = 24 + c * 2 + pair
+                added = jnp.where(row < 2, over_runs(packed[place]), over_runs(packed[12 + place]))
+                for p in (2 * pair, 2 * pair + 1):
+                    stress[c, p] = part[c, p] + added
+
+    @pl.when(level != 0)
+    def _():
+        for i, c in enumerate(RIM):
+            for p in range(PLANES):
+                stress[c, p, pl.ds(far_row, 4, stride=4), :] = edges[0, i, p]
+                stress[c, p, pl.ds(3 - far_row, 4, stride=4), :] = edges[1, i, p]
+                for r in (1, 2):
+                    own = part[c, p, pl.ds(r, 4, stride=4), :]
+                    stress[c, p, pl.ds(r, 4, stride=4), :] = own + packed[23 + (i * PLANES + p) * 2 + r]
+        for i, c in enumerate(REST):
+            for p in range(PLANES):
+                stress[c, p] = part[c, p] + rest[i, p]
+
     walls = [[stress[c, p] for p in range(PLANES)] for c in (0, 3, 4)]
     for p in range(PLANES):
         for a in range(3):
-            following, preceding = neighbours(core, [over_runs(from_mate[a, p])], [over_runs(from_far[a, p])])
-            rim = stress[RIM[a], p]
-            y_after = jnp.where(row == 3, following[0], pltpu.roll(rim, 15, 0))
-            y_before = jnp.where(row == 0, preceding[0], pltpu.roll(rim, 1, 0))
+            y_after, y_before = row_pair(
+                stress[RIM[a], p], row_edges(core, from_mate[a, p], from_far[a, p]), row
+            )
             x_after, x_before = plane_pair(walls[a], p)
             z_after, z_before = column_pair(stress[(4, 5, 2)[a], p], lane)
             force = (x_after - x_before) * 0.5 + (y_after - y_before) * 0.5 + (z_after - z_before) * 0.5
@@ -271,30 +312,38 @@
 
 
 def limit(mebibytes):
-    return pltpu.CompilerParams(vmem_limit_bytes=mebibytes * 2**20)
+    return pltpu.CompilerParams(vmem_limit_bytes=int(mebibytes * 2**20))
 
 
 def shape(*extent):
     return jax.ShapeDtypeStruct(extent, F32)
 
 
-def far_pairs(tiles):
+def far_pairs(tiles, across):
     pairs = []
     for l in range(2):
         for t in range(1, tiles, 2):
             u = (t + 1) % tiles
-            m = 1 - l if (t // 8) % 4 == 3 and t % 8 == 7 else l
+            m = 1 - l if across and (t // 8) % 4 == 3 and t % 8 == 7 else l
             pairs += [(l * tiles + t, m * tiles + u), (m * tiles + u, l * tiles + t)]
     return pairs
 
 
 def local(velocity, dumbbells, increments):
     tiles = lax.axis_size("tile")
-    far_swap = far_pairs(tiles)
+    far_swap = far_pairs(tiles, False)
+    rim_swap = far_pairs(tiles, True)
     mate_swap = [(t, t ^ 1) for t in range(tiles)]
     level_swap = [(0, 1), (1, 0)]
     vel = view(velocity)
-    far = lax.ppermute(vel, ("lvl", "tile"), far_swap)
+    toward_far = pl.pallas_call(
+        edge_kernel,
+        out_shape=shape(3, PLANES, 4, 128),
+        in_specs=[VMEM],
+        out_specs=VMEM,
+        compiler_params=limit(2),
+    )(vel)
+    far = lax.ppermute(toward_far, ("lvl", "tile"), far_swap)
     mate = lax.ppermute(vel, "tile", mate_swap)
     field = (3, PLANES, 16, 128)
     ensemble = (3, SAMPLES, PLANES, 16, 128)
@@ -308,35 +357,40 @@
             pltpu.SemaphoreType.DMA((SAMPLES,)),
             pltpu.SemaphoreType.DMA((SAMPLES,)),
         ],
-        compiler_params=limit(16),
+        compiler_params=limit(50.5),
     )(view(dumbbells[0]), view(increments[0]))
-    moved, part, toward, rest = pl.pallas_call(
+    moved, part, toward, packed = pl.pallas_call(
         advance_kernel,
-        out_shape=[shape(*ensemble), shape(6, PLANES, 16, 128), shape(2, 3, PLANES, 4, 128), shape(3, PLANES, 24, 128)],
+        out_shape=[
+            shape(*ensemble),
+            shape(6, PLANES, 16, 128),
+            shape(2, 3, PLANES, 4, 128),
+            shape(48, 4, 128),
+        ],
         in_specs=[VMEM] * 7,
         out_specs=[VMEM] * 4,
         compiler_params=limit(16),
     )(vel, mate, far, here, whole, first, later)
-    toward_other = lax.ppermute(toward, "lvl", level_swap)
-    rest_other = lax.ppermute(rest, "lvl", level_swap)
-    edges = toward + toward_other
-    from_far = lax.ppermute(edges[0], ("lvl", "tile"), far_swap)
-    from_mate = lax.ppermute(edges[1], "tile", mate_swap)
-    solvent, stored = pl.pallas_call(
+    packed_other = lax.ppermute(packed, "lvl", level_swap)
+    solvent, stored, rest = pl.pallas_call(
         momentum_kernel,
-        out_shape=[shape(*field), shape(*ensemble)],
-        in_specs=[VMEM] * 3 + [ANY],
-        out_specs=[VMEM, ANY],
+        out_shape=[shape(*field), shape(*ensemble), shape(*field)],
+        in_specs=[VMEM] * 3 + [ANY, VMEM],
+        out_specs=[VMEM, ANY, VMEM],
         scratch_shapes=[pltpu.SemaphoreType.DMA],
         compiler_params=limit(8),
-    )(vel, mate, far, moved)
+    )(vel, mate, far, moved, part)
+    rest_other = lax.ppermute(rest, "lvl", [(0, 1)])
+    edges = toward + packed_other[:24].reshape(toward.shape)
+    from_far = lax.ppermute(edges[0], ("lvl", "tile"), rim_swap)
+    from_mate = lax.ppermute(edges[1], "tile", mate_swap)
     velocity_next, stress = pl.pallas_call(
         final_kernel,
         out_shape=[shape(*field), shape(6, PLANES, 16, 128)],
-        in_specs=[VMEM] * 6,
+        in_specs=[VMEM] * 7,
         out_specs=[VMEM] * 2,
         compiler_params=limit(8),
-    )(solvent, part, rest_other, edges, from_far, from_mate)
+    )(solvent, part, packed_other, rest_other, edges, from_far, from_mate)
     return (unview(velocity_next), unview(stress), unview(stored)[None])
 
 

time: 35.7 us -> 32.4 us (0.908)
  waiting for transfers between devices: 11 us -> 2.59 us
  starting transfers between devices: 17.4 us -> 23.3 us
  local copies, waits for them, and re-layouts: 2.28 us -> 0.9 us
  Pallas kernels: 4.06 us -> 4.74 us
    ppermute x4, waiting for transfers between devices: 11 us -> 2.59 us  [the longest x1 1.66 us: local(): from_far = lax.ppermute(edges[0], ('lvl', 'tile'), rim_swap)]
    ppermute x4, starting transfers between devices: 17.3 us -> 23.1 us  [the longest x1 7.63 us: local(): far = lax.ppermute(toward_far, ('lvl', 'tile'), far_swap)]
    unnamed x6 -> x4, local copies, waits for them, and re-layouts: 2.27 us -> 0.89 us
    pallas_call x1, Pallas kernels: 1.24 us -> 1.83 us  [local(): pl.pallas_call(prepare_kernel, out_shape=[shape(*ensemble)] * 4, in_specs...]
  transfers between devices with their start and end apart: 6 -> 6, of which waited for: 2 -> 2; matrix products, arithmetic and copies ran while one was open for 0% -> 0% of each run, Pallas kernels for 6% -> 8%
where the time goes in v3:
time: 32.4 us; the launch traced here: 32.3 us
  starting transfers between devices  23.3 us (72%)
  Pallas kernels  4.74 us (15%)
  waiting for transfers between devices  2.59 us (8%)
  local copies, waits for them, and re-layouts  0.9 us (3%)
  between operations  0.73 us (2%)
    ppermute x1, starting transfers between devices, local(): far = lax.ppermute(toward_far, ('lvl', 'tile'), far_swap)  7.63 us
    ppermute x1, starting transfers between devices, local(): from_far = lax.ppermute(edges[0], ('lvl', 'tile'), rim_swap)  7.1 us
    ppermute x1, starting transfers between devices, local(): packed_other = lax.ppermute(packed, 'lvl', level_swap)  6.43 us
    ppermute x1, starting transfers between devices, local(): rest_other = lax.ppermute(rest, 'lvl', [(0, 1)])  1.93 us
    pallas_call x1, Pallas kernels, local(): pl.pallas_call(prepare_kernel, out_shape=[shape(*ensemble)] * 4, in_specs...  1.83 us
    ppermute x1, waiting for transfers between devices, local(): from_far = lax.ppermute(edges[0], ('lvl', 'tile'), rim_swap)  1.66 us
    pallas_call x1, Pallas kernels, local(): pl.pallas_call(advance_kernel, out_shape=[shape(*ensemble), shape(6, PLAN...  1.2 us
    ppermute x1, waiting for transfers between devices, local(): packed_other = lax.ppermute(packed, 'lvl', level_swap)  0.93 us
  transfers between devices with their start and end apart: 6, of which 2 were waited for; matrix products, arithmetic and copies ran while one was open for 0% of the time, Pallas kernels for 8%

profile of v3, /device:TPU:0, one launch (start us, length us, event | category | flops | bytes accessed | tf_op | source)
XLA Modules:
  0.0 32.3 jit_solution(6037666981006419185)
XLA Ops:
  0.6 0.1 collective-permute-start
  0.7 0.0 copy-start
  0.7 0.9 %copy-done = f32[3,4,4,512]{3,2,1,0:T(4,128)S(1)} copy-done((f32[3,4,4,512]{3,2,1,0:T(4,128)S(1)}, f32[3,4,4,512]{3,2,1,0:T(4,128)}, u32[]{:S(2)}) %copy-start) | copy-done | bytes 98328
  1.6 7.6 %collective-permute-start.1 = (f32[3,4,4,128]{3,2,1,0:T(4,128)S(1)}, f32[3,4,4,128]{3,2,1,0:T(4,128)S(1)}, u32[]{:S(2)}, u32[]{:S(2)}) collective-permute-start(f32[3,4,4,128]{3,2,1,0:T(4,128)S(1)} %shard_map.58), channel_id=1, source_target_pairs={{1,2},{2,1},{3,4},{4,3},{5,6},{6,5},{7,8},{8,7},{9,10},{10,9},{11,... | collective-permute-start | bytes 73736 | tf_op jit(solution)/shard_map/ppermute | solution.py:346
  9.3 0.0 copy-start.1
  9.3 1.8 %shard_map.59 = (f32[3,8,4,16,128]{4,3,2,1,0:T(8,128)S(1)}, f32[3,8,4,16,128]{4,3,2,1,0:T(8,128)S(1)}, f32[3,8,4,16,128]{4,3,2,1,0:T(8,128)S(1)}, f32[3,8,4,16,128]{4,3,2,1,0:T(8,128)S(1)}) custom-call(f32[3,8,4,16,128]{4,3,2,1,0:T(8,128)} %bitcast.39, bf16[2,3,8,4,16,128]{5,4,3,2,1,0:T(8,128)(2,1)} %bitcast.40), custom_call_target="tpu_custom_call" | custom-call | tf_op jit(solution)/shard_map/pallas_call | solution.py:350
  11.1 0.0 collective-permute-done.1.far
  11.1 0.0 collective-permute-done.mate
  11.1 0.0 copy-done.1
  11.1 1.2 %shard_map.60 = (f32[3,8,4,16,128]{4,3,2,1,0:T(8,128)S(1)}, f32[6,4,16,128]{3,2,1,0:T(8,128)S(1)}, f32[2,3,4,4,128]{4,3,2,1,0:T(4,128)S(1)}, f32[48,4,128]{2,1,0:T(4,128)S(1)}) custom-call(f32[3,4,16,128]{3,2,1,0:T(8,128)S(1)} %bitcast.37, f32[3,4,16,128]{3,2,1,0:T(8,128)S(1)} %collective-permute-done.mate, f32[3,4,4,128]{3,2,1,0:T(4,128)S(1)} %collective-permute-done.1.far, ...), custom_call_target="tpu_custom_call" | custom-call | tf_op jit(solution)/shard_map/pallas_call | solution.py:362
  12.3 6.4 %collective-permute-start.2 = (f32[48,4,128]{2,1,0:T(4,128)S(1)}, f32[48,4,128]{2,1,0:T(4,128)S(1)}, u32[]{:S(2)}, u32[]{:S(2)}) collective-permute-start(f32[48,4,128]{2,1,0:T(4,128)S(1)} %get-tuple-element.23), channel_id=1, source_target_pairs={{0,128},{128,0},{1,129},{129,1},{2,130},{130,2},{3,131},{131,3},{4... | collective-permute-start | bytes 294920 | tf_op jit(solution)/shard_map/ppermute | solution.py:374
  18.8 0.9 %shard_map.61 = (f32[3,4,16,128]{3,2,1,0:T(8,128)S(1)}, f32[3,8,4,16,128]{4,3,2,1,0:T(8,128)}, f32[3,4,16,128]{3,2,1,0:T(8,128)S(1)}) custom-call(f32[3,4,16,128]{3,2,1,0:T(8,128)S(1)} %bitcast.38, f32[3,4,16,128]{3,2,1,0:T(8,128)S(1)} %collective-permute-done.mate, f32[3,4,4,128]{3,2,1,0:T(4,128)S(1)} %collective-permute-done.1.far, ...), custom_call_target="tpu_custom_call" | custom-call | tf_op jit(solution)/shard_map/pallas_call | solution.py:375
  19.7 1.9 %collective-permute-start.3 = (f32[3,4,16,128]{3,2,1,0:T(8,128)S(1)}, f32[3,4,16,128]{3,2,1,0:T(8,128)S(1)}, u32[]{:S(2)}, u32[]{:S(2)}) collective-permute-start(f32[3,4,16,128]{3,2,1,0:T(8,128)S(1)} %get-tuple-element.24), channel_id=1, source_target_pairs={{0,128},{1,129},{2,130},{3,131},{4,132},{5,133},{6,134},{7,135},{8... | collective-permute-start | bytes 294920 | tf_op jit(solution)/shard_map/ppermute | solution.py:383
  21.6 0.9 %collective-permute-done.2.packed = f32[48,4,128]{2,1,0:T(4,128)S(1)} collective-permute-done((f32[48,4,128]{2,1,0:T(4,128)S(1)}, f32[48,4,128]{2,1,0:T(4,128)S(1)}, u32[]{:S(2)}, u32[]{:S(2)}) %collective-permute-start.2) | collective-permute-done | bytes 98336 | tf_op jit(solution)/shard_map/ppermute | solution.py:374
  22.6 0.1 collective-permute-start.5
  22.7 7.1 %collective-permute-start.4 = (f32[3,4,4,128]{3,2,1,0:T(4,128)S(1)}, f32[3,4,4,128]{3,2,1,0:T(4,128)S(1)}, u32[]{:S(2)}, u32[]{:S(2)}) collective-permute-start(f32[3,4,4,128]{3,2,1,0:T(4,128)S(1)} %get-tuple-element.30), channel_id=1, source_target_pairs={{1,2},{2,1},{3,4},{4,3},{5,6},{6,5},{7,8},{8,7},{9,10},{10,9},{11,... | collective-permute-start | bytes 73736 | tf_op jit(solution)/shard_map/ppermute | solution.py:385
  29.8 0.0 collective-permute-done.3.rest
  29.8 0.0 collective-permute-done.5.from_mate
  29.8 1.7 %collective-permute-done.4.from_far = f32[3,4,4,128]{3,2,1,0:T(4,128)S(1)} collective-permute-done((f32[3,4,4,128]{3,2,1,0:T(4,128)S(1)}, f32[3,4,4,128]{3,2,1,0:T(4,128)S(1)}, u32[]{:S(2)}, u32[]{:S(2)}) %collective-permute-start.4) | collective-permute-done | bytes 24608 | tf_op jit(solution)/shard_map/ppermute | solution.py:385
  31.4 0.8 %shard_map.62 = (f32[3,4,16,128]{3,2,1,0:T(8,128)}, f32[6,4,16,128]{3,2,1,0:T(8,128)}) custom-call(f32[3,4,16,128]{3,2,1,0:T(8,128)S(1)} %get-tuple-element.22.solvent, f32[6,4,16,128]{3,2,1,0:T(8,128)S(1)} %get-tuple-element.21.part, f32[48,4,128]{2,1,0:T(4,128)S(1)} %collective-permute-done.2.packed, f32[3,4,16,128]{3,2,1,0:T(8,128)S(1)} %collective-permute-done.3.rest, ...), custom_call_target="tpu_custom_call" | custom-call | tf_op jit(solution)/shard_map/pallas_call | solution.py:387
  (4 shorter events, 0.0 us)
Async XLA Ops:
  0.6 10.5 %collective-permute-start = (f32[3,4,16,128]{3,2,1,0:T(8,128)}, f32[3,4,16,128]{3,2,1,0:T(8,128)S(1)}, u32[]{:S(2)}, u32[]{:S(2)}) collective-permute-start(f32[3,4,16,128]{3,2,1,0:T(8,128)} %bitcast.35), channel_id=1, source_target_pairs={{0,1},{1,0},{2,3},{3,2},{4,5},{5,4},{6,7},{7,6},{8,9},{9,8},{10,11... | collective-permute-start | bytes 294920 | tf_op jit(solution)/shard_map/ppermute | solution.py:347
  0.7 0.9 %copy-start = (f32[3,4,4,512]{3,2,1,0:T(4,128)S(1)}, f32[3,4,4,512]{3,2,1,0:T(4,128)}, u32[]{:S(2)}) copy-start(f32[3,4,4,512]{3,2,1,0:T(4,128)} %param.3) | copy-start | bytes 294916
  1.6 9.5 %collective-permute-start.1 = (f32[3,4,4,128]{3,2,1,0:T(4,128)S(1)}, f32[3,4,4,128]{3,2,1,0:T(4,128)S(1)}, u32[]{:S(2)}, u32[]{:S(2)}) collective-permute-start(f32[3,4,4,128]{3,2,1,0:T(4,128)S(1)} %shard_map.58), channel_id=1, source_target_pairs={{1,2},{2,1},{3,4},{4,3},{5,6},{6,5},{7,8},{8,7},{9,10},{10,9},{11,... | collective-permute-start | bytes 73736 | tf_op jit(solution)/shard_map/ppermute | solution.py:346
  9.3 1.9 %copy-start.1 = (f32[3,4,4,512]{3,2,1,0:T(4,128)S(1)}, f32[3,4,4,512]{3,2,1,0:T(4,128)}, u32[]{:S(2)}) copy-start(f32[3,4,4,512]{3,2,1,0:T(4,128)} %param.3) | copy-start | bytes 294916
  12.3 10.2 %collective-permute-start.2 = (f32[48,4,128]{2,1,0:T(4,128)S(1)}, f32[48,4,128]{2,1,0:T(4,128)S(1)}, u32[]{:S(2)}, u32[]{:S(2)}) collective-permute-start(f32[48,4,128]{2,1,0:T(4,128)S(1)} %get-tuple-element.23), channel_id=1, source_target_pairs={{0,128},{128,0},{1,129},{129,1},{2,130},{130,2},{3,131},{131,3},{4... | collective-permute-start | bytes 294920 | tf_op jit(solution)/shard_map/ppermute | solution.py:374
  19.7 10.1 %collective-permute-start.3 = (f32[3,4,16,128]{3,2,1,0:T(8,128)S(1)}, f32[3,4,16,128]{3,2,1,0:T(8,128)S(1)}, u32[]{:S(2)}, u32[]{:S(2)}) collective-permute-start(f32[3,4,16,128]{3,2,1,0:T(8,128)S(1)} %get-tuple-element.24), channel_id=1, source_target_pairs={{0,128},{1,129},{2,130},{3,131},{4,132},{5,133},{6,134},{7,135},{8... | collective-permute-start | bytes 294920 | tf_op jit(solution)/shard_map/ppermute | solution.py:383
  22.6 7.2 %collective-permute-start.5 = (f32[3,4,4,128]{3,2,1,0:T(4,128)S(1)}, f32[3,4,4,128]{3,2,1,0:T(4,128)S(1)}, u32[]{:S(2)}, u32[]{:S(2)}) collective-permute-start(f32[3,4,4,128]{3,2,1,0:T(4,128)S(1)} %get-tuple-element.29), channel_id=1, source_target_pairs={{0,1},{1,0},{2,3},{3,2},{4,5},{5,4},{6,7},{7,6},{8,9},{9,8},{10,11... | collective-permute-start | bytes 73736 | tf_op jit(solution)/shard_map/ppermute | solution.py:386
  22.7 8.8 %collective-permute-start.4 = (f32[3,4,4,128]{3,2,1,0:T(4,128)S(1)}, f32[3,4,4,128]{3,2,1,0:T(4,128)S(1)}, u32[]{:S(2)}, u32[]{:S(2)}) collective-permute-start(f32[3,4,4,128]{3,2,1,0:T(4,128)S(1)} %get-tuple-element.30), channel_id=1, source_target_pairs={{1,2},{2,1},{3,4},{4,3},{5,6},{6,5},{7,8},{8,7},{9,10},{10,9},{11,... | collective-permute-start | bytes 73736 | tf_op jit(solution)/shard_map/ppermute | solution.py:385

commit v4 on v3

--- a/solution.py
+++ b/solution.py
@@ -75,6 +75,11 @@
     return following, preceding
 
 
+def beyond(edges, row):
+    following, preceding = edges
+    return jnp.where(row == 3, following, 0.0) - jnp.where(row == 0, preceding, 0.0)
+
+
 def row_edges(core, mate, far):
     mate, far = over_runs(mate), over_runs(far)
     return jnp.where(core == 0, mate, far), jnp.where(core == 0, far, mate)
@@ -117,7 +122,7 @@
             toward_far[a, p] = vel[a, p, pl.ds(far_row, 4, stride=4), :]
 
 
-def prepare_kernel(state, noise, here, whole, first, later, bring, state_sem, noise_sem):
+def prepare_kernel(state, noise, vel, here, whole, first, later, slopes, bring, state_sem, noise_sem):
     level = lax.axis_index("lvl")
 
     def copies(s):
@@ -129,6 +134,35 @@
     for s in range(SAMPLES):
         for copy in copies(s):
             copy.start()
+
+    row, lane = row_of(), lane_of()
+    velocity = [[vel[a, p] for p in range(PLANES)] for a in range(3)]
+    nothing = jnp.zeros((16, 128), F32)
+
+    def differences(a, p):
+        pairs = (
+            plane_pair(velocity[a], p),
+            row_pair(velocity[a][p], (nothing, nothing), row),
+            column_pair(velocity[a][p], lane),
+        )
+        return [(after - before) * 0.5 for after, before in pairs]
+
+    @pl.when(level == 0)
+    def _():
+        for a in range(3):
+            for p in range(PLANES):
+                for b, entry in enumerate(differences(a, p)):
+                    slopes[a, b, p] = STEP_TIME * entry
+
+    @pl.when(level != 0)
+    def _():
+        for a in range(3):
+            for pair in range(PLANES // 2):
+                lower, upper = differences(a, 2 * pair), differences(a, 2 * pair + 1)
+                for b in range(3):
+                    slopes[a, b, pair] = quad_sum(lower[b] + upper[b], row, lane) * (
+                        0.125 * 0.5 * STEP_TIME
+                    )
 
     def body(s, carry):
         for copy in copies(s):
@@ -154,22 +188,12 @@
     lax.fori_loop(0, SAMPLES, body, 0)
 
 
-def advance_kernel(vel, mate, far, state, whole, first, later, moved, part, toward, packed):
+def advance_kernel(slopes, mate, far, state, whole, first, later, moved, part, toward, packed):
     level = lax.axis_index("lvl")
     core = lax.rem(lax.axis_index("tile"), 2)
     row, lane = row_of(), lane_of()
-    velocity = [[vel[a, p] for p in range(PLANES)] for a in range(3)]
-
-    def gradient(p):
-        result = []
-        for a in range(3):
-            pairs = (
-                plane_pair(velocity[a], p),
-                row_pair(velocity[a][p], block_edges(core, mate[a, p], far[a, p]), row),
-                column_pair(velocity[a][p], lane),
-            )
-            result.append([(after - before) * 0.5 for after, before in pairs])
-        return result
+    def outer(a, p):
+        return beyond(block_edges(core, mate[a, p], far[a, p]), row)
 
     def emit(p, values):
         for c in range(6):
@@ -178,7 +202,9 @@
     @pl.when(level == 0)
     def _():
         for p in range(PLANES):
-            kappa = [[STEP_TIME * entry for entry in line] for line in gradient(p)]
+            kappa = [[slopes[a, b, p] for b in range(3)] for a in range(3)]
+            for a in range(3):
+                kappa[a][1] = kappa[a][1] + (0.5 * STEP_TIME) * outer(a, p)
 
             def body(s, sums, p=p, kappa=kappa):
                 pull = applied(kappa, [state[a, s, p] for a in range(3)])
@@ -193,11 +219,10 @@
     @pl.when(level != 0)
     def _():
         for pair in range(PLANES // 2):
-            lower, upper = gradient(2 * pair), gradient(2 * pair + 1)
-            kappa = [
-                [quad_sum(lower[a][b] + upper[a][b], row, lane) * (0.125 * 0.5 * STEP_TIME) for b in range(3)]
-                for a in range(3)
-            ]
+            kappa = [[slopes[a, b, pair] for b in range(3)] for a in range(3)]
+            for a in range(3):
+                edge = quad_sum(outer(a, 2 * pair) + outer(a, 2 * pair + 1), row, lane)
+                kappa[a][1] = kappa[a][1] + edge * (0.5 * 0.125 * 0.5 * STEP_TIME)
 
             def body(s, sums, pair=pair, kappa=kappa):
                 for p in (2 * pair, 2 * pair + 1):
@@ -271,7 +296,7 @@
     copy.wait()
 
 
-def final_kernel(solvent, part, packed, rest, edges, from_far, from_mate, velocity_next, stress):
+def stress_kernel(solvent, part, packed, rest, edges, inner, stress):
     level = lax.axis_index("lvl")
     core = lax.rem(lax.axis_index("tile"), 2)
     row, lane = row_of(), lane_of()
@@ -302,13 +327,21 @@
     walls = [[stress[c, p] for p in range(PLANES)] for c in (0, 3, 4)]
     for p in range(PLANES):
         for a in range(3):
-            y_after, y_before = row_pair(
-                stress[RIM[a], p], row_edges(core, from_mate[a, p], from_far[a, p]), row
-            )
+            nothing = jnp.zeros((16, 128), F32)
+            y_after, y_before = row_pair(stress[RIM[a], p], (nothing, nothing), row)
             x_after, x_before = plane_pair(walls[a], p)
             z_after, z_before = column_pair(stress[(4, 5, 2)[a], p], lane)
             force = (x_after - x_before) * 0.5 + (y_after - y_before) * 0.5 + (z_after - z_before) * 0.5
-            velocity_next[a, p] = solvent[a, p] + (STEP_TIME * POLYMER_WEIGHT) * force
+            inner[a, p] = solvent[a, p] + (STEP_TIME * POLYMER_WEIGHT) * force
+
+
+def final_kernel(inner, from_far, from_mate, velocity_next):
+    core = lax.rem(lax.axis_index("tile"), 2)
+    row = row_of()
+    for p in range(PLANES):
+        for a in range(3):
+            outer = beyond(row_edges(core, from_mate[a, p], from_far[a, p]), row)
+            velocity_next[a, p] = inner[a, p] + (0.5 * STEP_TIME * POLYMER_WEIGHT) * outer
 
 
 def limit(mebibytes):
@@ -347,18 +380,18 @@
     mate = lax.ppermute(vel, "tile", mate_swap)
     field = (3, PLANES, 16, 128)
     ensemble = (3, SAMPLES, PLANES, 16, 128)
-    here, whole, first, later = pl.pallas_call(
+    here, whole, first, later, slopes = pl.pallas_call(
         prepare_kernel,
-        out_shape=[shape(*ensemble)] * 4,
-        in_specs=[ANY] * 2,
-        out_specs=[VMEM] * 4,
+        out_shape=[shape(*ensemble)] * 4 + [shape(3, 3, PLANES, 16, 128)],
+        in_specs=[ANY] * 2 + [VMEM],
+        out_specs=[VMEM] * 5,
         scratch_shapes=[
             pltpu.VMEM((2,) + ensemble, jnp.bfloat16),
             pltpu.SemaphoreType.DMA((SAMPLES,)),
             pltpu.SemaphoreType.DMA((SAMPLES,)),
         ],
-        compiler_params=limit(50.5),
-    )(view(dumbbells[0]), view(increments[0]))
+        compiler_params=limit(50.2),
+    )(view(dumbbells[0]), view(increments[0]), vel)
     moved, part, toward, packed = pl.pallas_call(
         advance_kernel,
         out_shape=[
@@ -370,7 +403,7 @@
         in_specs=[VMEM] * 7,
         out_specs=[VMEM] * 4,
         compiler_params=limit(16),
-    )(vel, mate, far, here, whole, first, later)
+    )(slopes, mate, far, here, whole, first, later)
     packed_other = lax.ppermute(packed, "lvl", level_swap)
     solvent, stored, rest = pl.pallas_call(
         momentum_kernel,
@@ -384,13 +417,20 @@
     edges = toward + packed_other[:24].reshape(toward.shape)
     from_far = lax.ppermute(edges[0], ("lvl", "tile"), rim_swap)
     from_mate = lax.ppermute(edges[1], "tile", mate_swap)
-    velocity_next, stress = pl.pallas_call(
-        final_kernel,
+    inner, stress = pl.pallas_call(
+        stress_kernel,
         out_shape=[shape(*field), shape(6, PLANES, 16, 128)],
-        in_specs=[VMEM] * 7,
+        in_specs=[VMEM] * 5,
         out_specs=[VMEM] * 2,
         compiler_params=limit(8),
-    )(solvent, part, packed_other, rest_other, edges, from_far, from_mate)
+    )(solvent, part, packed_other, rest_other, edges)
+    velocity_next = pl.pallas_call(
+        final_kernel,
+        out_shape=shape(*field),
+        in_specs=[VMEM] * 3,
+        out_specs=VMEM,
+        compiler_params=limit(4),
+    )(inner, from_far, from_mate)
     return (unview(velocity_next), unview(stress), unview(stored)[None])
 
 

time: 32.4 us -> 32.2 us (level)
  waiting for transfers between devices: 2.59 us -> 1.92 us
    ppermute x1, waiting for transfers between devices: 1.66 us -> 0.96 us  [local(): from_far = lax.ppermute(edges[0], ('lvl', 'tile'), rim_swap)]
    pallas_call x2 -> x3, Pallas kernels: 2.63 us -> 3.2 us  [the longest x1 1.8 us: local(): pl.pallas_call(prepare_kernel, out_shape=[shape(*ensemble)] * 4 + [shape(...]
    pallas_call x1, Pallas kernels: 1.2 us -> 0.86 us  [local(): pl.pallas_call(advance_kernel, out_shape=[shape(*ensemble), shape(6, PLAN...]
  transfers between devices with their start and end apart: 6 -> 6, of which waited for: 2 -> 2; matrix products, arithmetic and copies ran while one was open for 0% -> 0% of each run, Pallas kernels for 8% -> 11%
where the time goes in v4:
time: 32.2 us; the launch traced here: 32 us
  starting transfers between devices  23.5 us (73%)
  Pallas kernels  4.97 us (15%)
  waiting for transfers between devices  1.92 us (6%)
  local copies, waits for them, and re-layouts  0.9 us (3%)
  between operations  0.72 us (2%)
    ppermute x1, starting transfers between devices, local(): far = lax.ppermute(toward_far, ('lvl', 'tile'), far_swap)  7.72 us
    ppermute x1, starting transfers between devices, local(): from_far = lax.ppermute(edges[0], ('lvl', 'tile'), rim_swap)  7.08 us
    ppermute x1, starting transfers between devices, local(): packed_other = lax.ppermute(packed, 'lvl', level_swap)  6.59 us
    ppermute x1, starting transfers between devices, local(): rest_other = lax.ppermute(rest, 'lvl', [(0, 1)])  1.93 us
    pallas_call x1, Pallas kernels, local(): pl.pallas_call(prepare_kernel, out_shape=[shape(*ensemble)] * 4 + [shape(...  1.8 us
    ppermute x1, waiting for transfers between devices, local(): from_far = lax.ppermute(edges[0], ('lvl', 'tile'), rim_swap)  0.96 us
    ppermute x1, waiting for transfers between devices, local(): packed_other = lax.ppermute(packed, 'lvl', level_swap)  0.95 us
    pallas_call x1, Pallas kernels, local(): pl.pallas_call(momentum_kernel, out_shape=[shape(*field), shape(*ensemble...  0.9 us
  transfers between devices with their start and end apart: 6, of which 2 were waited for; matrix products, arithmetic and copies ran while one was open for 0% of the time, Pallas kernels for 11%

profile of v4, /device:TPU:0, one launch (start us, length us, event | category | flops | bytes accessed | tf_op | source)
XLA Modules:
  0.0 32.0 jit_solution(12607765818603315558)
XLA Ops:
  0.6 0.1 collective-permute-start
  0.7 0.0 copy-start
  0.7 0.9 %copy-done = f32[3,4,4,512]{3,2,1,0:T(4,128)S(1)} copy-done((f32[3,4,4,512]{3,2,1,0:T(4,128)S(1)}, f32[3,4,4,512]{3,2,1,0:T(4,128)}, u32[]{:S(2)}) %copy-start) | copy-done | bytes 98328
  1.6 0.0 copy-start.1
  1.6 7.7 %collective-permute-start.1 = (f32[3,4,4,128]{3,2,1,0:T(4,128)S(1)}, f32[3,4,4,128]{3,2,1,0:T(4,128)S(1)}, u32[]{:S(2)}, u32[]{:S(2)}) collective-permute-start(f32[3,4,4,128]{3,2,1,0:T(4,128)S(1)} %shard_map.58), channel_id=1, source_target_pairs={{1,2},{2,1},{3,4},{4,3},{5,6},{6,5},{7,8},{8,7},{9,10},{10,9},{11,... | collective-permute-start | bytes 73736 | tf_op jit(solution)/shard_map/ppermute | solution.py:379
  9.4 0.0 copy-done.1
  9.4 1.8 %shard_map.59 = (f32[3,8,4,16,128]{4,3,2,1,0:T(8,128)S(1)}, f32[3,8,4,16,128]{4,3,2,1,0:T(8,128)S(1)}, f32[3,8,4,16,128]{4,3,2,1,0:T(8,128)S(1)}, f32[3,8,4,16,1...) custom-call(f32[3,8,4,16,128]{4,3,2,1,0:T(8,128)} %bitcast.39, bf16[2,3,8,4,16,128]{5,4,3,2,1,0:T(8,128)(2,1)} %bitcast.40, ...), custom_call_target="tpu_custom_call" | custom-call | tf_op jit(solution)/shard_map/pallas_call | solution.py:383
  11.2 0.0 collective-permute-done.1.far
  11.2 0.0 collective-permute-done.mate
  11.2 0.9 %shard_map.60 = (f32[3,8,4,16,128]{4,3,2,1,0:T(8,128)S(1)}, f32[6,4,16,128]{3,2,1,0:T(8,128)S(1)}, f32[2,3,4,4,128]{4,3,2,1,0:T(4,128)S(1)}, f32[48,4,128]{2,1,0:T(4,128)S(1)}) custom-call(f32[3,3,4,16,128]{4,3,2,1,0:T(8,128)S(1)} %get-tuple-element.17.slopes, f32[3,4,16,128]{3,2,1,0:T(8,128)S(1)} %collective-permute-done.mate, ...), custom_call_target="tpu_custom_call" | custom-call | tf_op jit(solution)/shard_map/pallas_call | solution.py:395
  12.1 6.6 %collective-permute-start.2 = (f32[48,4,128]{2,1,0:T(4,128)S(1)}, f32[48,4,128]{2,1,0:T(4,128)S(1)}, u32[]{:S(2)}, u32[]{:S(2)}) collective-permute-start(f32[48,4,128]{2,1,0:T(4,128)S(1)} %get-tuple-element.25), channel_id=1, source_target_pairs={{0,128},{128,0},{1,129},{129,1},{2,130},{130,2},{3,131},{131,3},{4... | collective-permute-start | bytes 294920 | tf_op jit(solution)/shard_map/ppermute | solution.py:407
  18.6 0.9 %shard_map.61 = (f32[3,4,16,128]{3,2,1,0:T(8,128)S(1)}, f32[3,8,4,16,128]{4,3,2,1,0:T(8,128)}, f32[3,4,16,128]{3,2,1,0:T(8,128)S(1)}) custom-call(f32[3,4,16,128]{3,2,1,0:T(8,128)S(1)} %bitcast.38, f32[3,4,16,128]{3,2,1,0:T(8,128)S(1)} %collective-permute-done.mate, f32[3,4,4,128]{3,2,1,0:T(4,128)S(1)} %collective-permute-done.1.far, ...), custom_call_target="tpu_custom_call" | custom-call | tf_op jit(solution)/shard_map/pallas_call | solution.py:408
  19.6 1.9 %collective-permute-start.3 = (f32[3,4,16,128]{3,2,1,0:T(8,128)S(1)}, f32[3,4,16,128]{3,2,1,0:T(8,128)S(1)}, u32[]{:S(2)}, u32[]{:S(2)}) collective-permute-start(f32[3,4,16,128]{3,2,1,0:T(8,128)S(1)} %get-tuple-element.26), channel_id=1, source_target_pairs={{0,128},{1,129},{2,130},{3,131},{4,132},{5,133},{6,134},{7,135},{8... | collective-permute-start | bytes 294920 | tf_op jit(solution)/shard_map/ppermute | solution.py:416
  21.5 1.0 %collective-permute-done.2.packed = f32[48,4,128]{2,1,0:T(4,128)S(1)} collective-permute-done((f32[48,4,128]{2,1,0:T(4,128)S(1)}, f32[48,4,128]{2,1,0:T(4,128)S(1)}, u32[]{:S(2)}, u32[]{:S(2)}) %collective-permute-start.2) | collective-permute-done | bytes 98336 | tf_op jit(solution)/shard_map/ppermute | solution.py:407
  22.5 0.1 collective-permute-start.5
  22.6 7.1 %collective-permute-start.4 = (f32[3,4,4,128]{3,2,1,0:T(4,128)S(1)}, f32[3,4,4,128]{3,2,1,0:T(4,128)S(1)}, u32[]{:S(2)}, u32[]{:S(2)}) collective-permute-start(f32[3,4,4,128]{3,2,1,0:T(4,128)S(1)} %get-tuple-element.32), channel_id=1, source_target_pairs={{1,2},{2,1},{3,4},{4,3},{5,6},{6,5},{7,8},{8,7},{9,10},{10,9},{11,... | collective-permute-start | bytes 73736 | tf_op jit(solution)/shard_map/ppermute | solution.py:418
  29.7 0.0 collective-permute-done.3.rest
  29.7 0.7 %shard_map.62 = (f32[3,4,16,128]{3,2,1,0:T(8,128)S(1)}, f32[6,4,16,128]{3,2,1,0:T(8,128)}) custom-call(f32[3,4,16,128]{3,2,1,0:T(8,128)S(1)} %get-tuple-element.24.solvent, f32[6,4,16,128]{3,2,1,0:T(8,128)S(1)} %get-tuple-element.23.part, f32[48,4,128]{2,1,0:T(4,128)S(1)} %collective-permute-done.2.packed, ...), custom_call_target="tpu_custom_call" | custom-call | tf_op jit(solution)/shard_map/pallas_call | solution.py:420
  30.4 0.0 collective-permute-done.5.from_mate
  30.4 1.0 %collective-permute-done.4.from_far = f32[3,4,4,128]{3,2,1,0:T(4,128)S(1)} collective-permute-done((f32[3,4,4,128]{3,2,1,0:T(4,128)S(1)}, f32[3,4,4,128]{3,2,1,0:T(4,128)S(1)}, u32[]{:S(2)}, u32[]{:S(2)}) %collective-permute-start.4) | collective-permute-done | bytes 24608 | tf_op jit(solution)/shard_map/ppermute | solution.py:418
  31.3 0.7 %shard_map.63 = f32[3,4,16,128]{3,2,1,0:T(8,128)} custom-call(f32[3,4,16,128]{3,2,1,0:T(8,128)S(1)} %get-tuple-element.28.inner, f32[3,4,4,128]{3,2,1,0:T(4,128)S(1)} %collective-permute-done.4.from_far, f32[3,4,4,128]{3,2,1,0:T(4,128)S(1)} %collective-permute-done.5.from_mate), custom_call_target="tpu_custom_call" | custom-call | tf_op jit(solution)/shard_map/pallas_call | solution.py:427
  (4 shorter events, 0.0 us)
Async XLA Ops:
  0.6 10.5 %collective-permute-start = (f32[3,4,16,128]{3,2,1,0:T(8,128)}, f32[3,4,16,128]{3,2,1,0:T(8,128)S(1)}, u32[]{:S(2)}, u32[]{:S(2)}) collective-permute-start(f32[3,4,16,128]{3,2,1,0:T(8,128)} %bitcast.35), channel_id=1, source_target_pairs={{0,1},{1,0},{2,3},{3,2},{4,5},{5,4},{6,7},{7,6},{8,9},{9,8},{10,11... | collective-permute-start | bytes 294920 | tf_op jit(solution)/shard_map/ppermute | solution.py:380
  0.7 0.9 %copy-start = (f32[3,4,4,512]{3,2,1,0:T(4,128)S(1)}, f32[3,4,4,512]{3,2,1,0:T(4,128)}, u32[]{:S(2)}) copy-start(f32[3,4,4,512]{3,2,1,0:T(4,128)} %param.3) | copy-start | bytes 294916
  1.6 7.7 %copy-start.1 = (f32[3,4,4,512]{3,2,1,0:T(4,128)S(1)}, f32[3,4,4,512]{3,2,1,0:T(4,128)}, u32[]{:S(2)}) copy-start(f32[3,4,4,512]{3,2,1,0:T(4,128)} %param.3) | copy-start | bytes 294916
  1.6 9.5 %collective-permute-start.1 = (f32[3,4,4,128]{3,2,1,0:T(4,128)S(1)}, f32[3,4,4,128]{3,2,1,0:T(4,128)S(1)}, u32[]{:S(2)}, u32[]{:S(2)}) collective-permute-start(f32[3,4,4,128]{3,2,1,0:T(4,128)S(1)} %shard_map.58), channel_id=1, source_target_pairs={{1,2},{2,1},{3,4},{4,3},{5,6},{6,5},{7,8},{8,7},{9,10},{10,9},{11,... | collective-permute-start | bytes 73736 | tf_op jit(solution)/shard_map/ppermute | solution.py:379
  12.1 10.4 %collective-permute-start.2 = (f32[48,4,128]{2,1,0:T(4,128)S(1)}, f32[48,4,128]{2,1,0:T(4,128)S(1)}, u32[]{:S(2)}, u32[]{:S(2)}) collective-permute-start(f32[48,4,128]{2,1,0:T(4,128)S(1)} %get-tuple-element.25), channel_id=1, source_target_pairs={{0,128},{128,0},{1,129},{129,1},{2,130},{130,2},{3,131},{131,3},{4... | collective-permute-start | bytes 294920 | tf_op jit(solution)/shard_map/ppermute | solution.py:407
  19.6 10.1 %collective-permute-start.3 = (f32[3,4,16,128]{3,2,1,0:T(8,128)S(1)}, f32[3,4,16,128]{3,2,1,0:T(8,128)S(1)}, u32[]{:S(2)}, u32[]{:S(2)}) collective-permute-start(f32[3,4,16,128]{3,2,1,0:T(8,128)S(1)} %get-tuple-element.26), channel_id=1, source_target_pairs={{0,128},{1,129},{2,130},{3,131},{4,132},{5,133},{6,134},{7,135},{8... | collective-permute-start | bytes 294920 | tf_op jit(solution)/shard_map/ppermute | solution.py:416
  22.5 7.9 %collective-permute-start.5 = (f32[3,4,4,128]{3,2,1,0:T(4,128)S(1)}, f32[3,4,4,128]{3,2,1,0:T(4,128)S(1)}, u32[]{:S(2)}, u32[]{:S(2)}) collective-permute-start(f32[3,4,4,128]{3,2,1,0:T(4,128)S(1)} %get-tuple-element.31), channel_id=1, source_target_pairs={{0,1},{1,0},{2,3},{3,2},{4,5},{5,4},{6,7},{7,6},{8,9},{9,8},{10,11... | collective-permute-start | bytes 73736 | tf_op jit(solution)/shard_map/ppermute | solution.py:419
  22.6 8.8 %collective-permute-start.4 = (f32[3,4,4,128]{3,2,1,0:T(4,128)S(1)}, f32[3,4,4,128]{3,2,1,0:T(4,128)S(1)}, u32[]{:S(2)}, u32[]{:S(2)}) collective-permute-start(f32[3,4,4,128]{3,2,1,0:T(4,128)S(1)} %get-tuple-element.32), channel_id=1, source_target_pairs={{1,2},{2,1},{3,4},{4,3},{5,6},{6,5},{7,8},{8,7},{9,10},{10,9},{11,... | collective-permute-start | bytes 73736 | tf_op jit(solution)/shard_map/ppermute | solution.py:418

commit v5 on v4

--- a/solution.py
+++ b/solution.py
@@ -68,13 +68,6 @@
     return jnp.concatenate([jnp.broadcast_to(rows[j : j + 1], (4, 128)) for j in range(4)], axis=0)
 
 
-def block_edges(core, mate, far):
-    rows = over_runs(far)
-    following = jnp.where(core == 0, pltpu.roll(mate, 3, 0), rows)
-    preceding = jnp.where(core == 0, rows, pltpu.roll(mate, 13, 0))
-    return following, preceding
-
-
 def beyond(edges, row):
     following, preceding = edges
     return jnp.where(row == 3, following, 0.0) - jnp.where(row == 0, preceding, 0.0)
@@ -115,11 +108,12 @@
     return [scaled[a] * state[b] for a, b in PAIRS]
 
 
-def edge_kernel(vel, toward_far):
+def edge_kernel(vel, toward_far, toward_mate):
     far_row = 3 * lax.rem(lax.axis_index("tile"), 2)
     for a in range(3):
         for p in range(PLANES):
             toward_far[a, p] = vel[a, p, pl.ds(far_row, 4, stride=4), :]
+            toward_mate[a, p] = vel[a, p, pl.ds(3 - far_row, 4, stride=4), :]
 
 
 def prepare_kernel(state, noise, vel, here, whole, first, later, slopes, bring, state_sem, noise_sem):
@@ -193,7 +187,7 @@
     core = lax.rem(lax.axis_index("tile"), 2)
     row, lane = row_of(), lane_of()
     def outer(a, p):
-        return beyond(block_edges(core, mate[a, p], far[a, p]), row)
+        return beyond(row_edges(core, mate[a, p], far[a, p]), row)
 
     def emit(p, values):
         for c in range(6):
@@ -284,7 +278,7 @@
             here = velocity[a][p]
             pairs = (
                 plane_pair(velocity[a], p),
-                row_pair(here, block_edges(core, mate[a, p], far[a, p]), row),
+                row_pair(here, row_edges(core, mate[a, p], far[a, p]), row),
                 column_pair(here, lane),
             )
             laplace = -6.0 * here
@@ -369,15 +363,15 @@
     mate_swap = [(t, t ^ 1) for t in range(tiles)]
     level_swap = [(0, 1), (1, 0)]
     vel = view(velocity)
-    toward_far = pl.pallas_call(
+    toward_far, toward_mate = pl.pallas_call(
         edge_kernel,
-        out_shape=shape(3, PLANES, 4, 128),
+        out_shape=[shape(3, PLANES, 4, 128)] * 2,
         in_specs=[VMEM],
-        out_specs=VMEM,
+        out_specs=[VMEM] * 2,
         compiler_params=limit(2),
     )(vel)
     far = lax.ppermute(toward_far, ("lvl", "tile"), far_swap)
-    mate = lax.ppermute(vel, "tile", mate_swap)
+    mate = lax.ppermute(toward_mate, "tile", mate_swap)
     field = (3, PLANES, 16, 128)
     ensemble = (3, SAMPLES, PLANES, 16, 128)
     here, whole, first, later, slopes = pl.pallas_call(

time: 32.2 us -> 32.2 us (level)
  no operation moved by 1% of the time
where the time goes in v5:
time: 32.2 us; the launch traced here: 32 us
  starting transfers between devices  23.5 us (73%)
  Pallas kernels  4.97 us (15%)
  waiting for transfers between devices  1.9 us (6%)
  local copies, waits for them, and re-layouts  0.9 us (3%)
  between operations  0.72 us (2%)
    ppermute x1, starting transfers between devices, local(): far = lax.ppermute(toward_far, ('lvl', 'tile'), far_swap)  7.64 us
    ppermute x1, starting transfers between devices, local(): from_far = lax.ppermute(edges[0], ('lvl', 'tile'), rim_swap)  7.05 us
    ppermute x1, starting transfers between devices, local(): packed_other = lax.ppermute(packed, 'lvl', level_swap)  6.67 us
    ppermute x1, starting transfers between devices, local(): rest_other = lax.ppermute(rest, 'lvl', [(0, 1)])  1.93 us
    pallas_call x1, Pallas kernels, local(): pl.pallas_call(prepare_kernel, out_shape=[shape(*ensemble)] * 4 + [shape(...  1.8 us
    ppermute x1, waiting for transfers between devices, local(): from_far = lax.ppermute(edges[0], ('lvl', 'tile'), rim_swap)  0.99 us
    ppermute x1, waiting for transfers between devices, local(): packed_other = lax.ppermute(packed, 'lvl', level_swap)  0.9 us
    pallas_call x1, Pallas kernels, local(): pl.pallas_call(momentum_kernel, out_shape=[shape(*field), shape(*ensemble...  0.9 us
  transfers between devices with their start and end apart: 6, of which 2 were waited for; matrix products, arithmetic and copies ran while one was open for 0% of the time, Pallas kernels for 11%

profile of v5, /device:TPU:0, one launch (start us, length us, event | category | flops | bytes accessed | tf_op | source)
XLA Modules:
  0.0 32.0 jit_solution(9546251431502420074)
XLA Ops:
  0.6 0.0 copy-start
  0.6 0.9 %copy-done = f32[3,4,4,512]{3,2,1,0:T(4,128)S(1)} copy-done((f32[3,4,4,512]{3,2,1,0:T(4,128)S(1)}, f32[3,4,4,512]{3,2,1,0:T(4,128)}, u32[]{:S(2)}) %copy-start) | copy-done | bytes 98328
  1.5 0.0 copy-start.1
  1.5 0.1 collective-permute-start
  1.6 7.6 %collective-permute-start.1 = (f32[3,4,4,128]{3,2,1,0:T(4,128)S(1)}, f32[3,4,4,128]{3,2,1,0:T(4,128)S(1)}, u32[]{:S(2)}, u32[]{:S(2)}) collective-permute-start(f32[3,4,4,128]{3,2,1,0:T(4,128)S(1)} %get-tuple-element.20), channel_id=1, source_target_pairs={{1,2},{2,1},{3,4},{4,3},{5,6},{6,5},{7,8},{8,7},{9,10},{10,9},{11,... | collective-permute-start | bytes 73736 | tf_op jit(solution)/shard_map/ppermute | solution.py:373
  9.3 0.0 copy-done.1
  9.3 1.8 %shard_map.59 = (f32[3,8,4,16,128]{4,3,2,1,0:T(8,128)S(1)}, f32[3,8,4,16,128]{4,3,2,1,0:T(8,128)S(1)}, f32[3,8,4,16,128]{4,3,2,1,0:T(8,128)S(1)}, f32[3,8,4,16,1...) custom-call(f32[3,8,4,16,128]{4,3,2,1,0:T(8,128)} %bitcast.38, bf16[2,3,8,4,16,128]{5,4,3,2,1,0:T(8,128)(2,1)} %bitcast.39, ...), custom_call_target="tpu_custom_call" | custom-call | tf_op jit(solution)/shard_map/pallas_call | solution.py:377
  11.1 0.0 collective-permute-done.mate
  11.1 0.0 collective-permute-done.1.far
  11.1 0.9 %shard_map.60 = (f32[3,8,4,16,128]{4,3,2,1,0:T(8,128)S(1)}, f32[6,4,16,128]{3,2,1,0:T(8,128)S(1)}, f32[2,3,4,4,128]{4,3,2,1,0:T(4,128)S(1)}, f32[48,4,128]{2,1,0:T(4,128)S(1)}) custom-call(f32[3,3,4,16,128]{4,3,2,1,0:T(8,128)S(1)} %get-tuple-element.21.slopes, f32[3,4,4,128]{3,2,1,0:T(4,128)S(1)} %collective-permute-done.mate, ...), custom_call_target="tpu_custom_call" | custom-call | tf_op jit(solution)/shard_map/pallas_call | solution.py:389
  12.0 6.7 %collective-permute-start.2 = (f32[48,4,128]{2,1,0:T(4,128)S(1)}, f32[48,4,128]{2,1,0:T(4,128)S(1)}, u32[]{:S(2)}, u32[]{:S(2)}) collective-permute-start(f32[48,4,128]{2,1,0:T(4,128)S(1)} %get-tuple-element.29), channel_id=1, source_target_pairs={{0,128},{128,0},{1,129},{129,1},{2,130},{130,2},{3,131},{131,3},{4... | collective-permute-start | bytes 294920 | tf_op jit(solution)/shard_map/ppermute | solution.py:401
  18.6 0.9 %shard_map.61 = (f32[3,4,16,128]{3,2,1,0:T(8,128)S(1)}, f32[3,8,4,16,128]{4,3,2,1,0:T(8,128)}, f32[3,4,16,128]{3,2,1,0:T(8,128)S(1)}) custom-call(f32[3,4,16,128]{3,2,1,0:T(8,128)S(1)} %bitcast.37, f32[3,4,4,128]{3,2,1,0:T(4,128)S(1)} %collective-permute-done.mate, f32[3,4,4,128]{3,2,1,0:T(4,128)S(1)} %collective-permute-done.1.far, ...), custom_call_target="tpu_custom_call" | custom-call | tf_op jit(solution)/shard_map/pallas_call | solution.py:402
  19.5 1.9 %collective-permute-start.3 = (f32[3,4,16,128]{3,2,1,0:T(8,128)S(1)}, f32[3,4,16,128]{3,2,1,0:T(8,128)S(1)}, u32[]{:S(2)}, u32[]{:S(2)}) collective-permute-start(f32[3,4,16,128]{3,2,1,0:T(8,128)S(1)} %get-tuple-element.30), channel_id=1, source_target_pairs={{0,128},{1,129},{2,130},{3,131},{4,132},{5,133},{6,134},{7,135},{8... | collective-permute-start | bytes 294920 | tf_op jit(solution)/shard_map/ppermute | solution.py:410
  21.5 0.9 %collective-permute-done.2.packed = f32[48,4,128]{2,1,0:T(4,128)S(1)} collective-permute-done((f32[48,4,128]{2,1,0:T(4,128)S(1)}, f32[48,4,128]{2,1,0:T(4,128)S(1)}, u32[]{:S(2)}, u32[]{:S(2)}) %collective-permute-start.2) | collective-permute-done | bytes 98336 | tf_op jit(solution)/shard_map/ppermute | solution.py:401
  22.4 0.1 collective-permute-start.5
  22.5 7.0 %collective-permute-start.4 = (f32[3,4,4,128]{3,2,1,0:T(4,128)S(1)}, f32[3,4,4,128]{3,2,1,0:T(4,128)S(1)}, u32[]{:S(2)}, u32[]{:S(2)}) collective-permute-start(f32[3,4,4,128]{3,2,1,0:T(4,128)S(1)} %get-tuple-element.36), channel_id=1, source_target_pairs={{1,2},{2,1},{3,4},{4,3},{5,6},{6,5},{7,8},{8,7},{9,10},{10,9},{11,... | collective-permute-start | bytes 73736 | tf_op jit(solution)/shard_map/ppermute | solution.py:412
  29.6 0.0 collective-permute-done.3.rest
  29.6 0.7 %shard_map.62 = (f32[3,4,16,128]{3,2,1,0:T(8,128)S(1)}, f32[6,4,16,128]{3,2,1,0:T(8,128)}) custom-call(f32[3,4,16,128]{3,2,1,0:T(8,128)S(1)} %get-tuple-element.28.solvent, f32[6,4,16,128]{3,2,1,0:T(8,128)S(1)} %get-tuple-element.27.part, f32[48,4,128]{2,1,0:T(4,128)S(1)} %collective-permute-done.2.packed, ...), custom_call_target="tpu_custom_call" | custom-call | tf_op jit(solution)/shard_map/pallas_call | solution.py:414
  30.3 0.0 collective-permute-done.5.from_mate
  30.3 1.0 %collective-permute-done.4.from_far = f32[3,4,4,128]{3,2,1,0:T(4,128)S(1)} collective-permute-done((f32[3,4,4,128]{3,2,1,0:T(4,128)S(1)}, f32[3,4,4,128]{3,2,1,0:T(4,128)S(1)}, u32[]{:S(2)}, u32[]{:S(2)}) %collective-permute-start.4) | collective-permute-done | bytes 24608 | tf_op jit(solution)/shard_map/ppermute | solution.py:412
  31.3 0.7 %shard_map.63 = f32[3,4,16,128]{3,2,1,0:T(8,128)} custom-call(f32[3,4,16,128]{3,2,1,0:T(8,128)S(1)} %get-tuple-element.32.inner, f32[3,4,4,128]{3,2,1,0:T(4,128)S(1)} %collective-permute-done.4.from_far, f32[3,4,4,128]{3,2,1,0:T(4,128)S(1)} %collective-permute-done.5.from_mate), custom_call_target="tpu_custom_call" | custom-call | tf_op jit(solution)/shard_map/pallas_call | solution.py:421
  (4 shorter events, 0.0 us)
Async XLA Ops:
  0.6 0.9 %copy-start = (f32[3,4,4,512]{3,2,1,0:T(4,128)S(1)}, f32[3,4,4,512]{3,2,1,0:T(4,128)}, u32[]{:S(2)}) copy-start(f32[3,4,4,512]{3,2,1,0:T(4,128)} %param.3) | copy-start | bytes 294916
  1.5 7.8 %copy-start.1 = (f32[3,4,4,512]{3,2,1,0:T(4,128)S(1)}, f32[3,4,4,512]{3,2,1,0:T(4,128)}, u32[]{:S(2)}) copy-start(f32[3,4,4,512]{3,2,1,0:T(4,128)} %param.3) | copy-start | bytes 294916
  1.5 9.5 %collective-permute-start = (f32[3,4,4,128]{3,2,1,0:T(4,128)S(1)}, f32[3,4,4,128]{3,2,1,0:T(4,128)S(1)}, u32[]{:S(2)}, u32[]{:S(2)}) collective-permute-start(f32[3,4,4,128]{3,2,1,0:T(4,128)S(1)} %get-tuple-element.19), channel_id=1, source_target_pairs={{0,1},{1,0},{2,3},{3,2},{4,5},{5,4},{6,7},{7,6},{8,9},{9,8},{10,11... | collective-permute-start | bytes 73736 | tf_op jit(solution)/shard_map/ppermute | solution.py:374
  1.6 9.5 %collective-permute-start.1 = (f32[3,4,4,128]{3,2,1,0:T(4,128)S(1)}, f32[3,4,4,128]{3,2,1,0:T(4,128)S(1)}, u32[]{:S(2)}, u32[]{:S(2)}) collective-permute-start(f32[3,4,4,128]{3,2,1,0:T(4,128)S(1)} %get-tuple-element.20), channel_id=1, source_target_pairs={{1,2},{2,1},{3,4},{4,3},{5,6},{6,5},{7,8},{8,7},{9,10},{10,9},{11,... | collective-permute-start | bytes 73736 | tf_op jit(solution)/shard_map/ppermute | solution.py:373
  12.0 10.4 %collective-permute-start.2 = (f32[48,4,128]{2,1,0:T(4,128)S(1)}, f32[48,4,128]{2,1,0:T(4,128)S(1)}, u32[]{:S(2)}, u32[]{:S(2)}) collective-permute-start(f32[48,4,128]{2,1,0:T(4,128)S(1)} %get-tuple-element.29), channel_id=1, source_target_pairs={{0,128},{128,0},{1,129},{129,1},{2,130},{130,2},{3,131},{131,3},{4... | collective-permute-start | bytes 294920 | tf_op jit(solution)/shard_map/ppermute | solution.py:401
  19.5 10.0 %collective-permute-start.3 = (f32[3,4,16,128]{3,2,1,0:T(8,128)S(1)}, f32[3,4,16,128]{3,2,1,0:T(8,128)S(1)}, u32[]{:S(2)}, u32[]{:S(2)}) collective-permute-start(f32[3,4,16,128]{3,2,1,0:T(8,128)S(1)} %get-tuple-element.30), channel_id=1, source_target_pairs={{0,128},{1,129},{2,130},{3,131},{4,132},{5,133},{6,134},{7,135},{8... | collective-permute-start | bytes 294920 | tf_op jit(solution)/shard_map/ppermute | solution.py:410
  22.4 7.9 %collective-permute-start.5 = (f32[3,4,4,128]{3,2,1,0:T(4,128)S(1)}, f32[3,4,4,128]{3,2,1,0:T(4,128)S(1)}, u32[]{:S(2)}, u32[]{:S(2)}) collective-permute-start(f32[3,4,4,128]{3,2,1,0:T(4,128)S(1)} %get-tuple-element.35), channel_id=1, source_target_pairs={{0,1},{1,0},{2,3},{3,2},{4,5},{5,4},{6,7},{7,6},{8,9},{9,8},{10,11... | collective-permute-start | bytes 73736 | tf_op jit(solution)/shard_map/ppermute | solution.py:413
  22.5 8.8 %collective-permute-start.4 = (f32[3,4,4,128]{3,2,1,0:T(4,128)S(1)}, f32[3,4,4,128]{3,2,1,0:T(4,128)S(1)}, u32[]{:S(2)}, u32[]{:S(2)}) collective-permute-start(f32[3,4,4,128]{3,2,1,0:T(4,128)S(1)} %get-tuple-element.36), channel_id=1, source_target_pairs={{1,2},{2,1},{3,4},{4,3},{5,6},{6,5},{7,8},{8,7},{9,10},{10,9},{11,... | collective-permute-start | bytes 73736 | tf_op jit(solution)/shard_map/ppermute | solution.py:412
